TPU v7x, 32 devices: a whole 2x2x4 slice. The times are simulated.
32 devices in a mesh: rep: 2 (over y), shard: 16 (over z, x, core).
Axes of the slice: x: 2, y: 2, z: 4, core: 2. Of those that a mesh axis runs over, the one named last changes fastest.
Arguments:
- tokens: bfloat16 [64, 256, 1152], P(('rep', 'shard')), may hold values from -6 to 6
- cotangent: bfloat16 [64, 256, 1152], P(('rep', 'shard')), may hold values from -6 to 6
- segments: int32 [64, 256], P(('rep', 'shard')), may hold values from 0 to 3, as said below
- norm_gains: float32 [4, 1152], replicated, may hold values from 0.5 to 1.5
- head_gains: float32 [2, 256], replicated, may hold values from 0.5 to 1.5
- qkv_weight: float32 [1152, 1536], P(None, 'shard'), may hold values from -0.1875 to 0.1875
- out_weight: float32 [1024, 1152], P('shard'), may hold values from -0.1875 to 0.1875
- gate_up_weight: float32 [1152, 13824], P(None, 'shard'), may hold values from -0.1875 to 0.1875
- down_weight: float32 [6912, 1152], P('shard'), may hold values from -0.078125 to 0.078125
- qkv_left: float32 [32, 9, 128, 128], P('shard'), as said below
- qkv_right: float32 [32, 9, 48, 48], P('shard'), as said below
- qkv_left_root: float32 [32, 9, 128, 128], P('shard'), as said below
- qkv_right_root: float32 [32, 9, 48, 48], P('shard'), as said below
- out_left: float32 [32, 9, 32, 32], P('shard'), as said below
- out_right: float32 [32, 9, 128, 128], P('shard'), as said below
- out_left_root: float32 [32, 9, 32, 32], P('shard'), as said below
- out_right_root: float32 [32, 9, 128, 128], P('shard'), as said below
- gate_up_left: float32 [32, 9, 128, 128], P('shard'), as said below
- gate_up_right: float32 [32, 9, 432, 432], P('shard'), as said below
- gate_up_left_root: float32 [32, 9, 128, 128], P('shard'), as said below
- gate_up_right_root: float32 [32, 9, 432, 432], P('shard'), as said below
- down_left: float32 [32, 9, 216, 216], P('shard'), as said below
- down_right: float32 [32, 9, 128, 128], P('shard'), as said below
- down_left_root: float32 [32, 9, 216, 216], P('shard'), as said below
- down_right_root: float32 [32, 9, 128, 128], P('shard'), as said below
- decay: float32 [4], replicated, may hold values from 0.4 to 0.6
- rate: float32 [4], replicated, may hold values from 0.02 to 0.2
Outputs:
- block_output: bfloat16 [64, 256, 1152], P(('rep', 'shard'))
- input_grad: float32 [64, 256, 1152], P(('rep', 'shard'))
- norm_gain_grad: float32 [4, 1152], P(None, 'shard')
- head_gain_grad: float32 [2, 256], P(None, 'shard')
- qkv_grad: float32 [1152, 1536], P(None, 'shard')
- out_grad: float32 [1024, 1152], P('shard')
- gate_up_grad: float32 [1152, 13824], P(None, 'shard')
- down_grad: float32 [6912, 1152], P('shard')
- qkv_new: float32 [1152, 1536], P(None, 'shard')
- out_new: float32 [1024, 1152], P('shard')
- gate_up_new: float32 [1152, 13824], P(None, 'shard')
- down_new: float32 [6912, 1152], P('shard')
- qkv_left_new: float32 [32, 9, 128, 128], P('shard')
- qkv_right_new: float32 [32, 9, 48, 48], P('shard')
- out_left_new: float32 [32, 9, 32, 32], P('shard')
- out_right_new: float32 [32, 9, 128, 128], P('shard')
- gate_up_left_new: float32 [32, 9, 128, 128], P('shard')
- gate_up_right_new: float32 [32, 9, 432, 432], P('shard')
- down_left_new: float32 [32, 9, 216, 216], P('shard')
- down_right_new: float32 [32, 9, 128, 128], P('shard')
Inputs may be any that keep to these rules, and one draw needn't show every extreme that they name: `segments`: in each group the prompt (segment 0) comes first with 64 to 128 tokens, then continuations 1 to 3 in order, each of 16 tokens or more. `qkv_left`: each block is symmetric positive definite. `qkv_right`: each block is symmetric positive definite. `qkv_left_root`: each block is symmetric positive definite. `qkv_right_root`: each block is symmetric positive definite. `out_left`: each block is symmetric positive definite. `out_right`: each block is symmetric positive definite. `out_left_root`: each block is symmetric positive definite. `out_right_root`: each block is symmetric positive definite. `gate_up_left`: each block is symmetric positive definite. `gate_up_right`: each block is symmetric positive definite. `gate_up_left_root`: each block is symmetric positive definite. `gate_up_right_root`: each block is symmetric positive definite. `down_left`: each block is symmetric positive definite. `down_right`: each block is symmetric positive definite. `down_left_root`: each block is symmetric positive definite. `down_right_root`: each block is symmetric positive definite.
All inputs are finite; a program needn't handle non-finite values.
Results may differ from a plain program's by a relative error of at most 0.024.
Values may be sent and summed in bfloat16 or wider, within the bound.
A program may use at most 384 MiB of HBM per device.

v0:
```python
import math

import jax
import jax.numpy as jnp
from jax import lax
from jax.sharding import PartitionSpec as P

HQ = 4
HD = 256
FF = 6912


epsilon = 1e-06
rope_base = 1000000.0
highest = lax.Precision.HIGHEST


def rms_norm(values, gains):
    return values * lax.rsqrt(jnp.mean(values * values, axis=-1, keepdims=True) + epsilon) * gains


def positions(segment_ids):
    length = segment_ids.shape[0]
    places = jnp.arange(length, dtype=jnp.int32)
    prompt = jnp.sum((segment_ids == 0).astype(jnp.int32))
    before = jnp.sum((segment_ids[None, :] < segment_ids[:, None]).astype(jnp.int32), axis=1)
    return jnp.where(segment_ids == 0, places, prompt + places - before)


def rope_tables(segment_ids):
    half = HD // 2
    spots = positions(segment_ids).astype(jnp.float32)
    freqs = jnp.exp(jnp.arange(half, dtype=jnp.float32) * (-2.0 * math.log(rope_base) / HD))
    angles = spots[:, None] * freqs[None, :]
    return (jnp.cos(angles), jnp.sin(angles))


def rotate(values, cosine, sine_part):
    half = values.shape[-1] // 2
    former = values[..., :half]
    latter = values[..., half:]
    return jnp.concatenate(
        [former * cosine - latter * sine_part, latter * cosine + former * sine_part], axis=-1
    )


def allowed_pairs(segment_ids):
    length = segment_ids.shape[0]
    places = jnp.arange(length, dtype=jnp.int32)
    causal = places[:, None] >= places[None, :]
    shared = (segment_ids[None, :] == 0) | (segment_ids[None, :] == segment_ids[:, None])
    return causal & shared


def split_heads(qkv, head_gains, cosine, sine_part):
    length = qkv.shape[0]
    query_rows = qkv[:, : HQ * HD].reshape(length, HQ, HD)
    key_rows = qkv[:, HQ * HD : (HQ + 1) * HD]
    value_rows = qkv[:, (HQ + 1) * HD :]
    query_rows = rotate(
        rms_norm(query_rows, head_gains[0]), cosine[:, None, :], sine_part[:, None, :]
    ) * HD ** (-0.5)
    key_rows = rotate(rms_norm(key_rows, head_gains[1]), cosine, sine_part)
    return (query_rows, key_rows, value_rows)


def geglu(gate_up):
    return jax.nn.gelu(gate_up[:, :FF], approximate=True) * gate_up[:, FF:]


def fetch_attn(qkv_weight, out_weight):
    return (
        lax.all_gather(qkv_weight.astype(jnp.bfloat16), "shard", axis=1, tiled=True),
        lax.all_gather(out_weight.astype(jnp.bfloat16), "shard", axis=0, tiled=True),
    )


def fetch_ffn(gate_up_weight, down_weight):
    return (
        lax.all_gather(gate_up_weight.astype(jnp.bfloat16), "shard", axis=1, tiled=True),
        lax.all_gather(down_weight.astype(jnp.bfloat16), "shard", axis=0, tiled=True),
    )


def fetch_attn_back(qkv_weight, out_weight):
    return (
        lax.all_gather(qkv_weight.astype(jnp.bfloat16), "shard", axis=1, tiled=True),
        lax.all_gather(out_weight.astype(jnp.bfloat16), "shard", axis=0, tiled=True),
    )


def fetch_ffn_back(gate_up_weight, down_weight):
    return (
        lax.all_gather(gate_up_weight.astype(jnp.bfloat16), "shard", axis=1, tiled=True),
        lax.all_gather(down_weight.astype(jnp.bfloat16), "shard", axis=0, tiled=True),
    )


def attention_scores(query_low, key_low, allowed):
    scores = jnp.einsum("thd,sd->hts", query_low, key_low, preferred_element_type=jnp.float32)
    return jnp.where(allowed[None], scores, -1000000000.0)


def forward_group(block_in, segment_ids, norm_gains, head_gains, attn_mats, ffn_mats):
    qkv_mat, out_mat = attn_mats
    gate_up_mat, down_mat = ffn_mats
    length = block_in.shape[0]
    cosine, sine_part = rope_tables(segment_ids)
    allowed = allowed_pairs(segment_ids)
    normed = rms_norm(block_in, norm_gains[0]).astype(jnp.bfloat16)
    qkv = jnp.dot(normed, qkv_mat, preferred_element_type=jnp.float32)
    query_rows, key_rows, value_rows = split_heads(qkv, head_gains, cosine, sine_part)
    query_low = query_rows.astype(jnp.bfloat16)
    key_low = key_rows.astype(jnp.bfloat16)
    value_low = value_rows.astype(jnp.bfloat16)
    scores = attention_scores(query_low, key_low, allowed)
    top_score = jnp.max(scores, axis=-1, keepdims=True)
    log_total = top_score + jnp.log(jnp.sum(jnp.exp(scores - top_score), axis=-1, keepdims=True))
    attn_probs = jnp.exp(scores - log_total).astype(jnp.bfloat16)
    context = jnp.einsum("hts,sd->thd", attn_probs, value_low, preferred_element_type=jnp.float32)
    context = context.reshape(length, HQ * HD).astype(jnp.bfloat16)
    attn_out = jnp.dot(context, out_mat, preferred_element_type=jnp.float32)
    middle = block_in + rms_norm(attn_out, norm_gains[1])
    normed_ffn = rms_norm(middle, norm_gains[2]).astype(jnp.bfloat16)
    gate_up = jnp.dot(normed_ffn, gate_up_mat, preferred_element_type=jnp.float32)
    hidden = geglu(gate_up).astype(jnp.bfloat16)
    ffn_out = jnp.dot(hidden, down_mat, preferred_element_type=jnp.float32)
    output = middle + rms_norm(ffn_out, norm_gains[3])
    saved = (
        normed,
        qkv,
        query_low,
        key_low,
        value_low,
        log_total,
        context,
        attn_out,
        middle,
        normed_ffn,
        gate_up,
        hidden,
        ffn_out,
    )
    return (output, saved)


def backward_group(
    block_in, segment_ids, grad_rows, norm_gains, head_gains, attn_mats, ffn_mats, saved
):
    qkv_mat, out_mat = attn_mats
    gate_up_mat, down_mat = ffn_mats
    (
        normed,
        qkv,
        query_low,
        key_low,
        value_low,
        log_total,
        context,
        attn_out,
        middle,
        normed_ffn,
        gate_up,
        hidden,
        ffn_out,
    ) = saved
    length = block_in.shape[0]
    cosine, sine_part = rope_tables(segment_ids)
    allowed = allowed_pairs(segment_ids)
    unused, pull_post = jax.vjp(rms_norm, ffn_out, norm_gains[3])
    ffn_grad, gain_three = pull_post(grad_rows)
    ffn_low = ffn_grad.astype(jnp.bfloat16)
    down_wgrad = jnp.einsum("tf,td->fd", hidden, ffn_low, preferred_element_type=jnp.float32)
    hidden_grad = jnp.einsum("td,fd->tf", ffn_low, down_mat, preferred_element_type=jnp.float32)
    unused, pull_geglu = jax.vjp(geglu, gate_up)
    (gate_up_grad,) = pull_geglu(hidden_grad)
    gate_up_low = gate_up_grad.astype(jnp.bfloat16)
    gate_up_wgrad = jnp.einsum(
        "td,tk->dk", normed_ffn, gate_up_low, preferred_element_type=jnp.float32
    )
    normed_ffn_grad = jnp.einsum(
        "tk,dk->td", gate_up_low, gate_up_mat, preferred_element_type=jnp.float32
    )
    unused, pull_pre = jax.vjp(rms_norm, middle, norm_gains[2])
    middle_part, gain_two = pull_pre(normed_ffn_grad)
    middle_grad = grad_rows + middle_part
    unused, pull_attn = jax.vjp(rms_norm, attn_out, norm_gains[1])
    attn_grad, gain_one = pull_attn(middle_grad)
    attn_low = attn_grad.astype(jnp.bfloat16)
    out_wgrad = jnp.einsum("tk,td->kd", context, attn_low, preferred_element_type=jnp.float32)
    context_grad = jnp.einsum("td,kd->tk", attn_low, out_mat, preferred_element_type=jnp.float32)
    context_grad = context_grad.astype(jnp.bfloat16).reshape(length, HQ, HD)
    scores = attention_scores(query_low, key_low, allowed)
    attn_probs = jnp.exp(scores - log_total)
    prob_grad = jnp.einsum(
        "thd,sd->hts", context_grad, value_low, preferred_element_type=jnp.float32
    )
    row_dot = jnp.sum(prob_grad * attn_probs, axis=-1, keepdims=True)
    score_grad = (attn_probs * (prob_grad - row_dot)).astype(jnp.bfloat16)
    query_grad = jnp.einsum("hts,sd->thd", score_grad, key_low, preferred_element_type=jnp.float32)
    key_grad = jnp.einsum("hts,thd->sd", score_grad, query_low, preferred_element_type=jnp.float32)
    value_grad = jnp.einsum(
        "hts,thd->sd",
        attn_probs.astype(jnp.bfloat16),
        context_grad,
        preferred_element_type=jnp.float32,
    )
    unused, pull_heads = jax.vjp(
        lambda rows, gains: split_heads(rows, gains, cosine, sine_part), qkv, head_gains
    )
    qkv_grad, head_grad = pull_heads((query_grad, key_grad, value_grad))
    qkv_low = qkv_grad.astype(jnp.bfloat16)
    qkv_wgrad = jnp.einsum("td,tk->dk", normed, qkv_low, preferred_element_type=jnp.float32)
    normed_grad = jnp.einsum("tk,dk->td", qkv_low, qkv_mat, preferred_element_type=jnp.float32)
    unused, pull_first = jax.vjp(rms_norm, block_in, norm_gains[0])
    first_part, gain_zero = pull_first(normed_grad)
    input_rows = middle_grad + first_part
    norm_grad = jnp.stack([gain_zero, gain_one, gain_two, gain_three])
    return (input_rows, (qkv_wgrad, out_wgrad, gate_up_wgrad, down_wgrad, norm_grad, head_grad))


def column_blocks(full, row_size, col_size):
    row_total, col_total = full.shape
    return full.reshape(row_total // row_size, row_size, col_total // col_size, col_size).transpose(
        2, 0, 1, 3
    )


def column_full(blocks):
    strip_count, row_count, row_size, col_size = blocks.shape
    return blocks.transpose(1, 2, 0, 3).reshape(row_count * row_size, strip_count * col_size)


def row_blocks(full, row_size, col_size):
    row_total, col_total = full.shape
    return full.reshape(row_total // row_size, row_size, col_total // col_size, col_size).transpose(
        0, 2, 1, 3
    )


def row_full(blocks):
    strip_count, col_count, row_size, col_size = blocks.shape
    return blocks.transpose(0, 2, 1, 3).reshape(strip_count * row_size, col_count * col_size)


def refresh(
    grad_blocks, weight_blocks, left_stat, right_stat, left_root, right_root, decay_rate, step_rate
):
    new_left = decay_rate * left_stat + (1.0 - decay_rate) * jnp.einsum(
        "sbij,sbkj->sbik", grad_blocks, grad_blocks, precision=highest
    )
    new_right = decay_rate * right_stat + (1.0 - decay_rate) * jnp.einsum(
        "sbji,sbjk->sbik", grad_blocks, grad_blocks, precision=highest
    )
    step = jnp.einsum(
        "sbij,sbjk->sbik",
        jnp.einsum("sbij,sbjk->sbik", left_root, grad_blocks, precision=highest),
        right_root,
        precision=highest,
    )
    return (weight_blocks - step_rate * step, new_left, new_right)


def per_device(
    tokens,
    cotangent,
    segments,
    norm_gains,
    head_gains,
    qkv_weight,
    out_weight,
    gate_up_weight,
    down_weight,
    qkv_left,
    qkv_right,
    qkv_left_root,
    qkv_right_root,
    out_left,
    out_right,
    out_left_root,
    out_right_root,
    gate_up_left,
    gate_up_right,
    gate_up_left_root,
    gate_up_right_root,
    down_left,
    down_right,
    down_left_root,
    down_right_root,
    decay,
    rate,
):
    micro_count = tokens.shape[0]
    outputs = []
    saved_all = []
    for batch_num in range(micro_count):
        block_in = tokens[batch_num].astype(jnp.float32)
        attn_mats = fetch_attn(qkv_weight, out_weight)
        ffn_mats = fetch_ffn(gate_up_weight, down_weight)
        output, saved = forward_group(
            block_in, segments[batch_num], norm_gains, head_gains, attn_mats, ffn_mats
        )
        outputs.append(output.astype(jnp.bfloat16))
        saved_all.append(saved)
    block_output = jnp.stack(outputs)
    input_rows_all = [None] * micro_count
    totals = None
    owned_sums = None
    for batch_num in reversed(range(micro_count)):
        block_in = tokens[batch_num].astype(jnp.float32)
        attn_mats = fetch_attn_back(qkv_weight, out_weight)
        ffn_mats = fetch_ffn_back(gate_up_weight, down_weight)
        grad_rows = cotangent[batch_num].astype(jnp.float32)
        input_rows, batch_grads = backward_group(
            block_in,
            segments[batch_num],
            grad_rows,
            norm_gains,
            head_gains,
            attn_mats,
            ffn_mats,
            saved_all[batch_num],
        )
        input_rows_all[batch_num] = input_rows
        totals = batch_grads if totals is None else jax.tree.map(jnp.add, totals, batch_grads)
    qkv_part, out_part, gate_up_part, down_part, norm_part, head_part = totals
    owned_sums = (
        lax.psum_scatter(
            qkv_part.astype(jnp.bfloat16), "shard", scatter_dimension=1, tiled=True
        ).astype(jnp.float32),
        lax.psum_scatter(
            out_part.astype(jnp.bfloat16), "shard", scatter_dimension=0, tiled=True
        ).astype(jnp.float32),
        lax.psum_scatter(
            gate_up_part.astype(jnp.bfloat16), "shard", scatter_dimension=1, tiled=True
        ).astype(jnp.float32),
        lax.psum_scatter(
            down_part.astype(jnp.bfloat16), "shard", scatter_dimension=0, tiled=True
        ).astype(jnp.float32),
        lax.psum_scatter(
            norm_part.astype(jnp.bfloat16), "shard", scatter_dimension=1, tiled=True
        ).astype(jnp.float32),
        lax.psum_scatter(
            head_part.astype(jnp.bfloat16), "shard", scatter_dimension=1, tiled=True
        ).astype(jnp.float32),
    )
    qkv_owned, out_owned, gate_up_owned, down_owned, norm_owned, head_owned = owned_sums
    summed = (
        lax.psum(qkv_owned.astype(jnp.bfloat16), "rep").astype(jnp.float32),
        lax.psum(out_owned.astype(jnp.bfloat16), "rep").astype(jnp.float32),
        lax.psum(gate_up_owned.astype(jnp.bfloat16), "rep").astype(jnp.float32),
        lax.psum(down_owned.astype(jnp.bfloat16), "rep").astype(jnp.float32),
        lax.psum(norm_owned.astype(jnp.bfloat16), "rep").astype(jnp.float32),
        lax.psum(head_owned.astype(jnp.bfloat16), "rep").astype(jnp.float32),
    )
    qkv_grad, out_grad, gate_up_grad, down_grad, norm_gain_grad, head_gain_grad = summed
    input_grad = jnp.stack(input_rows_all)
    total_tokens = micro_count * tokens.shape[1] * lax.axis_size("rep") * lax.axis_size("shard")
    scale = float(total_tokens) ** (-0.5)
    qkv_blocks, qkv_left_new, qkv_right_new = refresh(
        column_blocks(qkv_grad * scale, qkv_left.shape[-1], qkv_right.shape[-1]),
        column_blocks(qkv_weight, qkv_left.shape[-1], qkv_right.shape[-1]),
        qkv_left,
        qkv_right,
        qkv_left_root,
        qkv_right_root,
        decay[0],
        rate[0],
    )
    out_blocks, out_left_new, out_right_new = refresh(
        row_blocks(out_grad * scale, out_left.shape[-1], out_right.shape[-1]),
        row_blocks(out_weight, out_left.shape[-1], out_right.shape[-1]),
        out_left,
        out_right,
        out_left_root,
        out_right_root,
        decay[1],
        rate[1],
    )
    gate_up_blocks, gate_up_left_new, gate_up_right_new = refresh(
        column_blocks(gate_up_grad * scale, gate_up_left.shape[-1], gate_up_right.shape[-1]),
        column_blocks(gate_up_weight, gate_up_left.shape[-1], gate_up_right.shape[-1]),
        gate_up_left,
        gate_up_right,
        gate_up_left_root,
        gate_up_right_root,
        decay[2],
        rate[2],
    )
    down_blocks, down_left_new, down_right_new = refresh(
        row_blocks(down_grad * scale, down_left.shape[-1], down_right.shape[-1]),
        row_blocks(down_weight, down_left.shape[-1], down_right.shape[-1]),
        down_left,
        down_right,
        down_left_root,
        down_right_root,
        decay[3],
        rate[3],
    )
    return (
        block_output,
        input_grad,
        norm_gain_grad,
        head_gain_grad,
        qkv_grad,
        out_grad,
        gate_up_grad,
        down_grad,
        column_full(qkv_blocks),
        row_full(out_blocks),
        column_full(gate_up_blocks),
        row_full(down_blocks),
        qkv_left_new,
        qkv_right_new,
        out_left_new,
        out_right_new,
        gate_up_left_new,
        gate_up_right_new,
        down_left_new,
        down_right_new,
    )


def solution(mesh):
    return jax.shard_map(
        per_device,
        mesh=mesh,
        in_specs=(
            P(("rep", "shard"), None, None),
            P(("rep", "shard"), None, None),
            P(("rep", "shard"), None),
            P(),
            P(),
            P(None, "shard"),
            P("shard", None),
            P(None, "shard"),
            P("shard", None),
            P("shard", None, None, None),
            P("shard", None, None, None),
            P("shard", None, None, None),
            P("shard", None, None, None),
            P("shard", None, None, None),
            P("shard", None, None, None),
            P("shard", None, None, None),
            P("shard", None, None, None),
            P("shard", None, None, None),
            P("shard", None, None, None),
            P("shard", None, None, None),
            P("shard", None, None, None),
            P("shard", None, None, None),
            P("shard", None, None, None),
            P("shard", None, None, None),
            P("shard", None, None, None),
            P(),
            P(),
        ),
        out_specs=(
            P(("rep", "shard"), None, None),
            P(("rep", "shard"), None, None),
            P(None, "shard"),
            P(None, "shard"),
            P(None, "shard"),
            P("shard", None),
            P(None, "shard"),
            P("shard", None),
            P(None, "shard"),
            P("shard", None),
            P(None, "shard"),
            P("shard", None),
            P("shard", None, None, None),
            P("shard", None, None, None),
            P("shard", None, None, None),
            P("shard", None, None, None),
            P("shard", None, None, None),
            P("shard", None, None, None),
            P("shard", None, None, None),
            P("shard", None, None, None),
        ),
        check_vma=False,
    )
```

profile of v0, /device:TPU:0, one launch (start us, length us, event | category | flops | bytes accessed | tf_op | source)
XLA Modules:
  0.0 1459.0 jit_solution(17239118499376675944)
XLA Ops:
  25.6 35.2 %all-gather.5.cloned.1.call-done = bf16[1152,1536]{0,1:T(8,128)(2,1)} async-done(((bf16[1152,96]{0,1:T(8,128)(2,1)}), bf16[1152,1536]{0,1:T(8,128)(2,1)}) %all-gather.5.cloned.1.call-update) | async-done | bytes 3538960 | tf_op jit(solution)/shard_map/all_gather | solution.py:73
  99.4 5.6 all-gather.7.cloned.1.call-done
  112.7 153.4 %all-gather.9.cloned.1.call-done = bf16[1152,13824]{0,1:T(8,128)(2,1)} async-done(((bf16[1152,864]{0,1:T(8,128)(2,1)}), bf16[1152,13824]{0,1:T(8,128)(2,1)}) %all-gather.9.cloned.1.call-update) | async-done | bytes 31850512 | tf_op jit(solution)/shard_map/all_gather | solution.py:80
  266.1 20.9 %fusion.194 = f32[256,13824]{1,0:T(8,128)} fusion(bf16[1152,13824]{0,1:T(8,128)(2,1)} %all-gather.9.cloned.1.call-done, f32[256,1152]{1,0:T(8,128)} %get-tuple-element.153, f32[1152]{0:T(1024)S(1)} %get-tuple-element.133, f32[256]{0:T(256)S(1)} %fusion.171), kind=kOutput, calls=%fused_computation.360 | convolution fusion | flops 8154611712 | bytes 47191552 | tf_op jit(solution)/shard_map/dot_general | solution.py:125
  287.0 7.7 multiply_convert_fusion.1
  294.7 20.2 %fusion.195 = f32[256,13824]{1,0:T(8,128)} fusion(bf16[1152,13824]{0,1:T(8,128)(2,1)} %all-gather.9.cloned.1.call-done, f32[256,1152]{1,0:T(8,128)S(1)} %copy-done.17, f32[256]{0:T(256)S(1)} %fusion.176, f32[1152]{0:T(1024)S(1)} %get-tuple-element.133), kind=kOutput, calls=%fused_computation.361 | convolution fusion | flops 8154611712 | bytes 47191552 | tf_op jit(solution)/shard_map/dot_general | solution.py:125
  314.9 9.9 multiply_convert_fusion
  324.8 65.5 %all-gather.11.cloned.1.call-done = bf16[6912,1152]{1,0:T(8,128)(2,1)} async-done(((bf16[432,1152]{1,0:T(8,128)(2,1)}), bf16[6912,1152]{1,0:T(8,128)(2,1)}) %all-gather.11.cloned.1.call-update) | async-done | bytes 15925264 | tf_op jit(solution)/shard_map/all_gather | solution.py:81
  390.3 11.3 multiply_reduce_fusion.8
  410.8 17.3 %fusion.22 = (f32[256,6912]{1,0:T(8,128)}, f32[256,6912]{1,0:T(8,128)}) fusion(f32[256,13824]{1,0:T(8,128)} %fusion.195, bf16[256,1152]{1,0:T(8,128)(2,1)S(1)} %get-tuple-element.178, bf16[6912,1152]{1,0:T(8,128)(2,1)} %all-gather.11.cloned.1.call-done), kind=kOutput, calls=%fused_computation.40 | convolution fusion | flops 4115791872 | bytes 44826624 | tf_op jit(solution)/shard_map/td,fd->tf/dot_general | solution.py:174
  428.1 16.8 %fusion.21 = (f32[256,6912]{1,0:T(8,128)}, f32[256,6912]{1,0:T(8,128)}) fusion(f32[256,13824]{1,0:T(8,128)} %fusion.194, bf16[256,1152]{1,0:T(8,128)(2,1)S(1)} %get-tuple-element.171, bf16[6912,1152]{1,0:T(8,128)(2,1)} %all-gather.11.cloned.1.call-done), kind=kOutput, calls=%fused_computation.39 | convolution fusion | flops 4115791872 | bytes 44826624 | tf_op jit(solution)/shard_map/td,fd->tf/dot_general | solution.py:174
  444.9 20.7 %fusion.83 = f32[256,1152]{1,0:T(8,128)} fusion(bf16[1152,13824]{0,1:T(8,128)(2,1)} %all-gather.9.cloned.1.call-done, f32[256,6912]{1,0:T(8,128)} %get-tuple-element.159, f32[256,6912]{1,0:T(8,128)} %get-tuple-element.158), kind=kOutput, calls=%fused_computation.183 | convolution fusion | flops 8160804864 | bytes 47185920 | tf_op jit(solution)/shard_map/tk,dk->td/dot_general | solution.py:181
  465.6 22.4 %multiply_reduce_fusion = (f32[1152]{0:T(1024)}, f32[256]{0:T(256)}, f32[256]{0:T(256)}, f32[1152]{0:T(1024)}, f32[256,1152]{1,0:T(8,128)}) fusion(f32[256,1152]{1,0:T(8,128)} %get-tuple-element.153, f32[256]{0:T(256)} %copy-done.97, f32[1152]{0:T(1024)S(1)} %get-tuple-element.133, f32[256,1152]{1,0:T(8,128)} %get-tuple-element.180, ...), kind=kOutput, calls=%fused_computation.134 | convolution fusion | flops 8164341760 | bytes 50742784 | tf_op jit(solution)/shard_map/tk,dk->td/dot_general | solution.py:181
  534.4 15.2 %fusion.203 = f32[6912,1152]{1,0:T(8,128)} fusion(bf16[256,6912]{1,0:T(8,128)(2,1)} %multiply_convert_fusion, bf16[256,1152]{1,0:T(8,128)(2,1)S(1)} %copy-done.54), kind=kOutput, calls=%fused_computation.369 | convolution fusion | flops 4076863488 | bytes 35979264 | tf_op jit(solution)/shard_map/tf,td->fd/dot_general | solution.py:173
  549.6 18.4 %fusion.1 = bf16[6912,1152]{1,0:T(8,128)(2,1)} fusion(f32[6912,1152]{1,0:T(8,128)} %fusion.203, bf16[256,6912]{1,0:T(8,128)(2,1)S(1)} %copy-done.21, bf16[256,1152]{1,0:T(8,128)(2,1)S(1)} %copy-done.52), kind=kOutput, calls=%fused_computation.3 | convolution fusion | flops 4092788736 | bytes 51904512 | tf_op jit(solution)/shard_map/tf,td->fd/dot_general | solution.py:173
  568.5 29.7 %fusion.82 = f32[1152,13824]{0,1:T(8,128)} fusion(f32[256,6912]{1,0:T(8,128)} %get-tuple-element.159, f32[256,6912]{1,0:T(8,128)} %get-tuple-element.158, f32[256,1152]{1,0:T(8,128)} %get-tuple-element.180, f32[256]{0:T(256)} %copy-done.98, f32[1152]{0:T(1024)S(1)} %get-tuple-element.133), kind=kOutput, calls=%fused_computation.182 | convolution fusion | flops 8161689600 | bytes 79042048 | tf_op jit(solution)/shard_map/td,tk->dk/dot_general | solution.py:178
  598.2 40.5 %fusion = bf16[1152,13824]{0,1:T(8,128)(2,1)} fusion(f32[1152,13824]{0,1:T(8,128)} %fusion.82, f32[256,6912]{1,0:T(8,128)} %get-tuple-element.157, f32[256,6912]{1,0:T(8,128)} %get-tuple-element.156, f32[256,1152]{1,0:T(8,128)S(1)} %copy-done.16, f32[1152]{0:T(1024)S(1)} %get-tuple-element.133, f32[256]{0:T(256)} %copy-done.97), kind=kOutput, calls=%fused_computation.1 | convolution fusion | flops 8193540096 | bytes 110892544 | tf_op jit(solution)/shard_map/td,tk->dk/dot_general | solution.py:178
  642.4 176.0 %reduce-scatter.15.cloned.1.call-done = bf16[432,1152]{1,0:T(8,128)(2,1)} async-done(((bf16[6912,1152]{1,0:T(8,128)(2,1)}), bf16[432,1152]{1,0:T(8,128)(2,1)}) %reduce-scatter.15.cloned.1.call-update) | async-done | bytes 995344 | tf_op jit(solution)/shard_map/reduce_scatter | solution.py:337
  818.4 324.4 %reduce-scatter.13.cloned.1.call-done = bf16[1152,864]{0,1:T(8,128)(2,1)} async-done(((bf16[1152,13824]{0,1:T(8,128)(2,1)}), bf16[1152,864]{0,1:T(8,128)(2,1)}) %reduce-scatter.13.cloned.1.call-update) | async-done | bytes 1990672 | tf_op jit(solution)/shard_map/reduce_scatter | solution.py:334
  1145.6 6.2 reshape.669
  1168.3 33.3 %all-reduce.22 = bf16[4,1152]{1,0:T(4,128)(2,1)} all-reduce(bf16[4,1152]{1,0:T(4,128)(2,1)} %fusion.163), channel_id=2, replica_groups=mesh['rep'=2,'shard'=16] {'shard'}, use_global_device_ids=true, to_apply=%region_42.43.clone | all-reduce | flops 4608 | bytes 18432
  1210.8 5.2 all-reduce.23
  1217.1 73.5 %all-reduce.27.cloned.1.call-done = (bf16[1152,96]{0,1:T(8,128)(2,1)}, bf16[64,1152]{1,0:T(8,128)(2,1)}, bf16[1152,864]{0,1:T(8,128)(2,1)}, bf16[432,1152]{1,0:T(8,128)(2,1)}) async-done(((bf16[1152,96]{0,1:T(8,128)(2,1)}, bf16[64,1152]{1,0:T(8,128)(2,1)}, bf16[1152,864]{0,1:T(8,128)(2,1)}, bf16[432,1152]{1,0:T(8,128)(2,1)}), (bf16[1152,96]{0,1:T(8,128)(2,1)}, bf16[64,1152]{1,0:T(8,128)(2,1)}, ...) | async-done | bytes 3354640 | tf_op jit(solution)/shard_map/psum | solution.py:349
  1294.2 5.4 broadcast_multiply_fusion
  1315.9 6.2 reshape.670
  1322.1 7.2 fusion.18
  1329.3 35.1 %bitcast_subtract_fusion = f32[9,128,2,432]{1,3,0,2:T(8,128)S(1)} fusion(f32[9,128,2,432]{1,0,3,2:T(8,128)} %reshape.669, f32[2,9,432,128]{3,2,1,0:T(8,128)S(1)} %fusion.18, f32[2,9,432,432]{3,2,1,0:T(8,128)} %param.47, f32[]{:T(128)} %bitcast.53), kind=kOutput, calls=%fused_computation.31 | convolution fusion | flops 5161771008 | bytes 25380868 | tf_op jit(solution)/shard_map/sbij,sbjk->sbik/dot_general | solution.py:255
  1371.8 7.5 fusion.26
  1399.0 11.5 fusion.47
  1410.5 27.1 %multiply_add_fusion = f32[2,9,432,432]{3,2,1,0:T(8,128)} fusion(f32[2,9,432,432]{3,2,1,0:T(8,128)} %param.45, f32[]{:T(128)S(6)} %sub.148, f32[]{:T(128)} %bitcast.61, f32[9,128,2,432]{1,0,3,2:T(8,128)} %reshape.670), kind=kOutput, calls=%fused_computation.4 | convolution fusion | flops 5169858048 | bytes 30855176 | tf_op jit(solution)/shard_map/sbji,sbjk->sbik/dot_general | solution.py:252
  1437.7 7.9 multiply_add_fusion.1
  1445.6 6.4 fusion.44
  (516 shorter events, 195.8 us)
Async XLA Ops:
  7.2 1314.9 %copy-start = (f32[2,9,128,128]{3,2,1,0:T(8,128)S(1)}, f32[2,9,128,128]{3,2,1,0:T(8,128)}, u32[]{:S(2)}) copy-start(f32[2,9,128,128]{3,2,1,0:T(8,128)} %param.46) | copy-start | bytes 3538948
  7.2 53.6 %all-gather.5.cloned.1.call-start = ((), (), s32[]{:S(2)}) async-start(), calls=%async_computation.5 | async-start | bytes 3760128 | tf_op jit(solution)/shard_map/all_gather | solution.py:73
  9.1 95.9 %all-gather.7.cloned.1.call-start = ((), (), s32[]{:S(2)}) async-start(), calls=%async_computation.6 | async-start | bytes 2506752 | tf_op jit(solution)/shard_map/all_gather | solution.py:74
  10.8 255.3 %all-gather.9.cloned.1.call-start = ((), (), s32[]{:S(2)}) async-start(), calls=%async_computation.7 | async-start | bytes 33841152 | tf_op jit(solution)/shard_map/all_gather | solution.py:80
  14.5 375.7 %all-gather.11.cloned.1.call-start = ((), (), s32[]{:S(2)}) async-start(), calls=%async_computation.8 | async-start | bytes 16920576 | tf_op jit(solution)/shard_map/all_gather | solution.py:81
  17.3 623.0 %reduce-scatter.11.cloned.1.call-start = ((), (), s32[]{:S(2)}) async-start(), calls=%async_computation.10 | async-start | bytes 2506752 | tf_op jit(solution)/shard_map/reduce_scatter | solution.py:331
  19.9 50.5 %copy-start.94 = (f32[1152]{0:T(1024)}, f32[1152]{0:T(1024)S(1)}, u32[]{:S(2)}) copy-start(f32[1152]{0:T(1024)S(1)} %get-tuple-element.132) | copy-start | bytes 13828
  20.4 43.6 %copy-start.145 = (f32[256]{0:T(256)}, f32[256]{0:T(256)S(1)}, u32[]{:S(2)}) copy-start(f32[256]{0:T(256)S(1)} %get-tuple-element.126) | copy-start | bytes 3076
  20.4 43.6 %copy-start.146 = (f32[256]{0:T(256)}, f32[256]{0:T(256)S(1)}, u32[]{:S(2)}) copy-start(f32[256]{0:T(256)S(1)} %get-tuple-element.127) | copy-start | bytes 3076
  20.4 43.6 %copy-start.132 = (f32[256]{0:T(256)}, f32[256]{0:T(256)S(1)}, u32[]{:S(2)}) copy-start(f32[256]{0:T(256)S(1)} %fusion.168) | copy-start | bytes 3076
  112.6 174.3 %copy-start.143 = (f32[256]{0:T(256)}, f32[256]{0:T(256)S(1)}, u32[]{:S(2)}) copy-start(f32[256]{0:T(256)S(1)} %get-tuple-element.179) | copy-start | bytes 3076
  112.7 174.3 %copy-start.144 = (f32[256]{0:T(256)}, f32[256]{0:T(256)S(1)}, u32[]{:S(2)}) copy-start(f32[256]{0:T(256)S(1)} %get-tuple-element.152) | copy-start | bytes 3076
  112.7 153.4 %copy-start.97 = (f32[256]{0:T(256)}, f32[256]{0:T(256)S(1)}, u32[]{:S(2)}) copy-start(f32[256]{0:T(256)S(1)} %fusion.171) | copy-start | bytes 3076
  112.7 182.0 %copy-start.98 = (f32[256]{0:T(256)}, f32[256]{0:T(256)S(1)}, u32[]{:S(2)}) copy-start(f32[256]{0:T(256)S(1)} %fusion.176) | copy-start | bytes 3076
  390.3 11.3 copy-start.20
  390.3 12.3 copy-start.164
  410.8 17.3 %copy-start.53 = (bf16[256,1152]{1,0:T(8,128)(2,1)}, bf16[256,1152]{1,0:T(8,128)(2,1)S(1)}, u32[]{:S(2)}) copy-start(bf16[256,1152]{1,0:T(8,128)(2,1)S(1)} %get-tuple-element.178) | copy-start | bytes 1769476
  410.8 17.3 %copy-start.51 = (bf16[256,1152]{1,0:T(8,128)(2,1)}, bf16[256,1152]{1,0:T(8,128)(2,1)S(1)}, u32[]{:S(2)}) copy-start(bf16[256,1152]{1,0:T(8,128)(2,1)S(1)} %get-tuple-element.171) | copy-start | bytes 1769476
  465.6 23.8 %copy-start.12 = (f32[256,1152]{1,0:T(8,128)S(1)}, f32[256,1152]{1,0:T(8,128)}, u32[]{:S(2)}) copy-start(f32[256,1152]{1,0:T(8,128)} %copy-done.11) | copy-start | bytes 3538948
  465.6 23.8 %copy-start.14 = (f32[256,1152]{1,0:T(8,128)S(1)}, f32[256,1152]{1,0:T(8,128)}, u32[]{:S(2)}) copy-start(f32[256,1152]{1,0:T(8,128)} %copy-done.13) | copy-start | bytes 3538948
  509.3 133.1 %reduce-scatter.9.cloned.1.call-start = ((), (), s32[]{:S(2)}) async-start(), calls=%async_computation.9 | async-start | bytes 3760128 | tf_op jit(solution)/shard_map/reduce_scatter | solution.py:328
  533.4 16.2 %copy-start.52 = (bf16[256,1152]{1,0:T(8,128)(2,1)S(1)}, bf16[256,1152]{1,0:T(8,128)(2,1)}, u32[]{:S(2)}) copy-start(bf16[256,1152]{1,0:T(8,128)(2,1)} %copy-done.51) | copy-start | bytes 1769476
  533.4 285.0 %reduce-scatter.15.cloned.1.call-start = ((), (), s32[]{:S(2)}) async-start(), calls=%async_computation.12 | async-start | bytes 16920576 | tf_op jit(solution)/shard_map/reduce_scatter | solution.py:337
  534.4 15.2 %copy-start.21 = (bf16[256,6912]{1,0:T(8,128)(2,1)S(1)}, bf16[256,6912]{1,0:T(8,128)(2,1)}, u32[]{:S(2)}) copy-start(bf16[256,6912]{1,0:T(8,128)(2,1)} %multiply_convert_fusion.1) | copy-start | bytes 10616836
  568.1 30.2 %copy-start.16 = (f32[256,1152]{1,0:T(8,128)S(1)}, f32[256,1152]{1,0:T(8,128)}, u32[]{:S(2)}) copy-start(f32[256,1152]{1,0:T(8,128)} %get-tuple-element.153) | copy-start | bytes 3538948
  568.1 574.7 %reduce-scatter.13.cloned.1.call-start = ((), (), s32[]{:S(2)}) async-start(), calls=%async_computation.11 | async-start | bytes 33841152 | tf_op jit(solution)/shard_map/reduce_scatter | solution.py:334
  638.8 571.2 %reduce-scatter.17.cloned.1.call-start = ((), (), s32[]{:S(2)}) async-start(), calls=%async_computation.13 | async-start | bytes 69632
  640.3 650.3 %all-reduce.27.cloned.1.call-start = ((), (), s32[]{:S(2)}) async-start(), calls=%async_computation.14 | async-start | bytes 6709248 | tf_op jit(solution)/shard_map/psum | solution.py:349
  1167.6 38.5 %copy-start.23 = (f32[256,1152]{1,0:T(8,128)S(1)}, f32[256,1152]{1,0:T(8,128)}, u32[]{:S(2)}) copy-start(f32[256,1152]{1,0:T(8,128)} %copy-done.22) | copy-start | bytes 3538948
  1384.3 14.8 %slice-start = ((s8[7077888]{0:T(1024)(128)(4,1)}), s8[4194304]{0:T(1024)(128)(4,1)S(1)}, s32[]{:S(2)}) async-start(s8[7077888]{0:T(1024)(128)(4,1)} %bitcast.274), calls=%async_computation.15 | async-start | bytes 8388608
  1386.5 12.5 slice-start.1
  1410.5 27.1 %copy-start.8 = (f32[2,216,9,128]{3,2,1,0:T(8,128)S(1)}, f32[2,216,9,128]{3,2,1,0:T(8,128)}, u32[]{:S(2)}) copy-start(f32[2,216,9,128]{3,2,1,0:T(8,128)} %reshape.673) | copy-start | bytes 5971972
  (147 other events, 459.6 us)
Sparse Core Ops, SparseCore 0:
  10.9 49.8 all-gather.4
  63.7 41.3 all-gather.6
  107.2 158.8 all-gather.8
  268.7 121.5 all-gather.10
  509.4 61.0 reduce-scatter.10
  575.3 67.0 reduce-scatter.8
  647.7 170.7 reduce-scatter.14
  823.3 319.4 reduce-scatter.12
  1147.1 51.0 reduce-scatter.16
  1200.6 90.0 all-reduce.26
where the time goes:
time: 1470 us; the launch traced here: 1460 us
  waiting for transfers between devices  836 us (57%)
  matrix products  405 us (28%)
  other arithmetic  86.2 us (6%)
  local copies, waits for them, and re-layouts  72.3 us (5%)
  blocking collectives  38.4 us (3%)
  between operations  19.8 us (1%)
    reduce_scatter x1, waiting for transfers between devices, per_device(): lax.psum_scatter(gate_up_part.astype(jnp.bfloat16), 'shard', scatter_dime...  324 us
    reduce_scatter x1, waiting for transfers between devices, per_device(): lax.psum_scatter(down_part.astype(jnp.bfloat16), 'shard', scatter_dimensi...  176 us
    all_gather x1, waiting for transfers between devices, fetch_ffn(): lax.all_gather(gate_up_weight.astype(jnp.bfloat16), 'shard', axis=1, tile...  153 us
    psum x1, waiting for transfers between devices, per_device(): lax.psum(qkv_owned.astype(jnp.bfloat16), 'rep').astype(jnp.float32)  73.5 us
    dot_general x2, matrix products, backward_group(): jnp.einsum('td,tk->dk', normed_ffn, gate_up_low, preferred_element_type=j...  70.2 us
    all_gather x1, waiting for transfers between devices, fetch_ffn(): lax.all_gather(down_weight.astype(jnp.bfloat16), 'shard', axis=0, tiled=T...  65.5 us
    dot_general x4, matrix products, refresh(): jnp.einsum('sbij,sbjk->sbik', jnp.einsum('sbij,sbjk->sbik', left_root, gr...  44.1 us
    dot_general x2, matrix products, backward_group(): jnp.einsum('tk,dk->td', gate_up_low, gate_up_mat, preferred_element_type=...  43.1 us
  transfers between devices with their start and end apart: 10, of which 8 were waited for; matrix products, arithmetic and copies ran while one was open for 19% of the time, Pallas kernels for 0%

commit v1 on v0

v1 whole, which is shorter than its diff:
```python
import math

import jax
import jax.numpy as jnp
from jax import lax
from jax.sharding import PartitionSpec as P

HQ = 4
HD = 256
AXES = ("rep", "shard")
PAD = 16

epsilon = 1e-06
rope_base = 1000000.0
low = jnp.bfloat16
full = jnp.float32


def dot(a, b, ca, cb):
    return lax.dot_general(a, b, (((ca,), (cb,)), ((), ())), preferred_element_type=full)


class Place:
    def __init__(self, mesh):
        self.reps = mesh.shape["rep"]
        self.shards = mesh.shape["shard"]
        self.chips = self.shards // 2
        self.outer = min(4, self.chips)
        self.inner = self.chips // self.outer

    def here(self):
        r, i = lax.axis_index("rep"), lax.axis_index("shard")
        chip = i // 2
        return r % 2, chip // self.inner, chip % self.inner, i % 2

    def send(self, value, where):
        pairs = []
        for r in range(self.reps):
            for i in range(self.shards):
                o, n, c = i // 2 // self.inner, i // 2 % self.inner, i % 2
                to = where(r, o, n, c)
                if to is not None:
                    r2, o2, n2, c2 = to
                    pairs.append((r * self.shards + i, r2 * self.shards + (o2 * self.inner + n2) * 2 + c2))
        return lax.ppermute(value, AXES, pairs)

    def swap_rep(self, value):
        return self.send(value, lambda r, o, n, c: (r ^ 1, o, n, c))

    def swap_core(self, value):
        return self.send(value, lambda r, o, n, c: (r, o, n, 1 - c))

    def line(self, value, size, move, index):
        up, down = [], []
        send_up = send_down = value
        for k in range(size - 1):
            send_up = move(send_up, 1)
            send_down = move(send_down, -1)
            up.append(send_up)
            down.append(send_down)
        window = jnp.stack(up[::-1] + [value] + down)
        return lax.dynamic_slice_in_dim(window, size - 1 - index, size, 0)

    def move_outer(self, value, by, keep=None):
        def where(r, o, n, c):
            if keep is not None and not keep(n, c):
                return None
            return (r, o + by, n, c) if 0 <= o + by < self.outer else None

        return self.send(value, where)

    def move_inner(self, value, by, keep=None):
        def where(r, o, n, c):
            if keep is not None and not keep(n, c):
                return None
            return (r, o, n + by, c) if 0 <= n + by < self.inner else None

        return self.send(value, where)

    def gather_outer(self, value, keep=None):
        o = self.here()[1]
        return self.line(value, self.outer, lambda v, by: self.move_outer(v, by, keep), o)

    def gather_chips(self, value):
        n = self.here()[2]
        columns = self.gather_outer(value)
        if self.inner == 2:
            other = self.send(columns, lambda r, o, n, c: (r, o, 1 - n, c))
            both = jnp.where(n == 0, jnp.stack([columns, other], 1), jnp.stack([other, columns], 1))
        else:
            both = jnp.swapaxes(self.line(columns, self.inner, self.move_inner, n), 0, 1)
        return both.reshape((self.chips,) + value.shape)

    def scatter_line(self, parts, size, move, index):
        zeros = jnp.zeros_like(parts[:1])
        padded = jnp.concatenate([zeros] * (size - 1) + [parts] + [zeros] * (size - 1), 0)

        def part(offset):
            return lax.dynamic_index_in_dim(padded, index + offset + size - 1, 0, keepdims=False)

        sums = []
        for way in (1, -1):
            got = None
            for k in range(size - 1, 0, -1):
                mine = part(way * k)
                if got is not None:
                    mine = (mine.astype(full) + got.astype(full)).astype(low)
                got = move(mine, way)
            sums.append(got)
        return (part(0).astype(full) + sums[0].astype(full) + sums[1].astype(full)).astype(low)

    def scatter_outer(self, parts, keep=None):
        o = self.here()[1]
        return self.scatter_line(parts, self.outer, lambda v, by: self.move_outer(v, by, keep), o)

    def scatter_chips(self, parts):
        n = self.here()[2]
        parts = parts.reshape((self.outer, self.inner) + parts.shape[1:])
        if self.inner == 2:
            away = lax.dynamic_index_in_dim(parts, 1 - n, 1, keepdims=False)
            mine = lax.dynamic_index_in_dim(parts, n, 1, keepdims=False)
            got = self.send(away, lambda r, o, n, c: (r, o, 1 - n, c))
            column = (mine.astype(full) + got.astype(full)).astype(low)
        else:
            column = self.scatter_line(jnp.swapaxes(parts, 0, 1), self.inner, self.move_inner, n)
        return self.scatter_outer(column)

    def gather_down(self, block):
        par, o, n, c = self.here()
        other = self.swap_core(block)
        mine = jnp.where(par == c, block, other)
        if self.inner == 2:
            keep = lambda n, c: n == c
            column = self.gather_outer(mine, keep)
            got = self.send(column, lambda r, o, n, c: (r, o, 1 - n, c) if n == c else None)
            return jnp.where(n == c, column, got)
        both = self.gather_chips(mine)
        both = both.reshape((self.chips // 2, 2) + block.shape)
        return lax.dynamic_index_in_dim(both, c, 1, keepdims=False)

    def scatter_down(self, parts):
        par, o, n, c = self.here()
        if self.inner == 2:
            keep = lambda n, c: n == c
            got = self.send(parts, lambda r, o, n, c: (r, o, 1 - n, c) if n != c else None)
            column = (parts.astype(full) + got.astype(full)).astype(low)
            own = self.scatter_outer(column, keep)
        else:
            zeros = jnp.zeros_like(parts)
            both = jnp.where(c == 0, jnp.stack([parts, zeros], 1), jnp.stack([zeros, parts], 1))
            own = self.scatter_chips(both.reshape((self.chips,) + parts.shape[1:]))
        own = self.sum_pairs(own)
        far = self.send(own, lambda r, o, n, c: (r ^ 1, o, n, r % 2) if c == n % 2 else None)
        near = self.send(own, lambda r, o, n, c: (r, o, n, r % 2) if c == n % 2 and c != r % 2 else None)
        return jnp.where(c != par, far, jnp.where(c == n % 2, own, near))

    def sum_pairs(self, value):
        if self.reps == 2:
            return value
        groups = [list(range(k, self.reps, 2)) for k in range(2)]
        return lax.psum(value, "rep", axis_index_groups=groups)

    def gather_tokens(self, rows):
        two = jnp.concatenate([rows, self.swap_rep(rows)], 0)
        return jnp.concatenate([two, self.swap_core(two)], 0)

    def scatter_tokens(self, rows):
        half, quarter = rows.shape[0] // 2, rows.shape[0] // 4
        two = rows[:half] + self.swap_core(rows[half:].astype(low)).astype(full)
        return two[:quarter] + self.swap_rep(two[quarter:].astype(low)).astype(full)


def rms_norm(values, gains):
    return values * lax.rsqrt(jnp.mean(values * values, axis=-1, keepdims=True) + epsilon) * gains


def positions(segment_ids):
    length = segment_ids.shape[0]
    places = jnp.arange(length, dtype=jnp.int32)
    prompt = jnp.sum((segment_ids == 0).astype(jnp.int32))
    before = jnp.sum((segment_ids[None, :] < segment_ids[:, None]).astype(jnp.int32), axis=1)
    return jnp.where(segment_ids == 0, places, prompt + places - before)


def rope_tables(segment_ids):
    half = HD // 2
    spots = positions(segment_ids).astype(full)
    freqs = jnp.exp(jnp.arange(half, dtype=full) * (-2.0 * math.log(rope_base) / HD))
    angles = spots[:, None] * freqs[None, :]
    return (jnp.cos(angles), jnp.sin(angles))


def rotate(values, cosine, sine_part):
    half = values.shape[-1] // 2
    former = values[..., :half]
    latter = values[..., half:]
    return jnp.concatenate(
        [former * cosine - latter * sine_part, latter * cosine + former * sine_part], axis=-1
    )


def allowed_pairs(segment_ids):
    length = segment_ids.shape[0]
    places = jnp.arange(length, dtype=jnp.int32)
    causal = places[:, None] >= places[None, :]
    shared = (segment_ids[None, :] == 0) | (segment_ids[None, :] == segment_ids[:, None])
    return causal & shared


def split_heads(qkv, head_gains, cosine, sine_part):
    length = qkv.shape[0]
    query_rows = qkv[:, : HQ * HD].reshape(length, HQ, HD)
    key_rows = qkv[:, HQ * HD : (HQ + 1) * HD]
    value_rows = qkv[:, (HQ + 1) * HD :]
    query_rows = rotate(
        rms_norm(query_rows, head_gains[0]), cosine[:, None, :], sine_part[:, None, :]
    ) * HD ** (-0.5)
    key_rows = rotate(rms_norm(key_rows, head_gains[1]), cosine, sine_part)
    return (query_rows, key_rows, value_rows)


def attend(query_low, key_low, value_low, allowed):
    scores = jnp.einsum("thd,sd->hts", query_low, key_low, preferred_element_type=full)
    scores = jnp.where(allowed[None], scores, -1000000000.0)
    exponent = jnp.exp(scores - jnp.max(scores, axis=-1, keepdims=True))
    probs = exponent / jnp.sum(exponent, axis=-1, keepdims=True)
    context = jnp.einsum("hts,sd->thd", probs.astype(low), value_low, preferred_element_type=full)
    return probs, context.reshape(context.shape[0], HQ * HD).astype(low)


def attend_back(context_grad, probs, query_low, key_low, value_low):
    context_grad = context_grad.reshape(context_grad.shape[0], HQ, HD)
    prob_grad = jnp.einsum("thd,sd->hts", context_grad, value_low, preferred_element_type=full)
    row_dot = jnp.sum(prob_grad * probs, axis=-1, keepdims=True)
    score_grad = (probs * (prob_grad - row_dot)).astype(low)
    query_grad = jnp.einsum("hts,sd->thd", score_grad, key_low, preferred_element_type=full)
    key_grad = jnp.einsum("hts,thd->sd", score_grad, query_low, preferred_element_type=full)
    value_grad = jnp.einsum("hts,thd->sd", probs.astype(low), context_grad, preferred_element_type=full)
    return query_grad, key_grad, value_grad


def gelu_parts(gate):
    c = math.sqrt(2.0 / math.pi)
    t = jnp.tanh(c * (gate + 0.044715 * gate * gate * gate))
    cdf = 0.5 * (1.0 + t)
    slope = cdf + 0.5 * gate * (1.0 - t * t) * (c * (1.0 + 3.0 * 0.044715 * gate * gate))
    return gate * cdf, slope


def column_blocks(whole, row_size, col_size):
    rows, cols = whole.shape
    return whole.reshape(rows // row_size, row_size, cols // col_size, col_size).transpose(2, 0, 1, 3)


def column_full(blocks):
    strips, count, row_size, col_size = blocks.shape
    return blocks.transpose(1, 2, 0, 3).reshape(count * row_size, strips * col_size)


def row_blocks(whole, row_size, col_size):
    rows, cols = whole.shape
    return whole.reshape(rows // row_size, row_size, cols // col_size, col_size).transpose(0, 2, 1, 3)


def row_full(blocks):
    strips, count, row_size, col_size = blocks.shape
    return blocks.transpose(0, 2, 1, 3).reshape(strips * row_size, count * col_size)


def refresh(grads, weights, left_stat, right_stat, left_root, right_root, decay_rate, step_rate):
    def mul(spec, a, b):
        return jnp.einsum(spec, a.astype(low), b.astype(low), preferred_element_type=full)

    new_left = decay_rate * left_stat + (1.0 - decay_rate) * mul("sbij,sbkj->sbik", grads, grads)
    new_right = decay_rate * right_stat + (1.0 - decay_rate) * mul("sbji,sbjk->sbik", grads, grads)
    step = mul("sbij,sbjk->sbik", mul("sbij,sbjk->sbik", left_root, grads), right_root)
    return (weights - step_rate * step, new_left, new_right)


def per_device(place, tokens, cotangent, segments, norm_gains, head_gains, *rest):
    qkv_weight, out_weight, gate_up_weight, down_weight = rest[:4]
    stats = rest[4:20]
    decay, rate = rest[20:]
    groups, length, width = tokens.shape
    par, outer, inner, core = place.here()
    qw, ow = qkv_weight.shape[1], out_weight.shape[0]
    unit = down_weight.shape[0]

    attn_own = jnp.concatenate([qkv_weight.T, out_weight], 0).astype(low)
    both = place.gather_chips(attn_own)
    mate = place.swap_core(both)
    both = jnp.where(core == 0, jnp.stack([both, mate], 1), jnp.stack([mate, both], 1))
    qkv_mat = both[:, :, :qw].reshape(place.shards * qw, width)
    out_mat = both[:, :, qw:].reshape(place.shards * ow, width)
    gate_up_own = lax.dynamic_index_in_dim(
        gate_up_weight.T.astype(low).reshape(2, unit, width), par, 0, keepdims=False
    )
    gate_up_all = place.gather_chips(gate_up_own)
    hidden_count = place.chips // 2 * unit
    gate_mat = gate_up_all[: place.chips // 2].reshape(hidden_count, width)
    up_mat = gate_up_all[place.chips // 2 :].reshape(hidden_count, width)
    down_mat = place.gather_down(down_weight.astype(low)).reshape(hidden_count, width)

    block_in = tokens.astype(full).reshape(groups * length, width)
    cosine, sine_part = jax.vmap(rope_tables)(segments)
    allowed = jax.vmap(allowed_pairs)(segments)
    normed = rms_norm(block_in, norm_gains[0]).astype(low)
    qkv = dot(normed, qkv_mat, 1, 1).reshape(groups, length, -1)
    query_rows, key_rows, value_rows = jax.vmap(split_heads, (0, None, 0, 0))(
        qkv, head_gains, cosine, sine_part
    )
    query_low, key_low, value_low = query_rows.astype(low), key_rows.astype(low), value_rows.astype(low)
    probs, context = jax.vmap(attend)(query_low, key_low, value_low, allowed)
    context = context.reshape(groups * length, HQ * HD)
    attn_out = dot(context, out_mat, 1, 0)
    middle = block_in + rms_norm(attn_out, norm_gains[1])
    normed_ffn = rms_norm(middle, norm_gains[2]).astype(low)
    normed_all = place.gather_tokens(normed_ffn)
    gate = dot(normed_all, gate_mat, 1, 1)
    up = dot(normed_all, up_mat, 1, 1)
    act, slope = gelu_parts(gate)
    hidden = (act * up).astype(low)
    up_factor = act.astype(low)
    gate_factor = (slope * up).astype(low)
    ffn_out = place.scatter_tokens(dot(hidden, down_mat, 1, 0))
    block_output = (middle + rms_norm(ffn_out, norm_gains[3])).astype(low).reshape(tokens.shape)

    grad_rows = cotangent.astype(full).reshape(groups * length, width)
    unused, pull_post = jax.vjp(rms_norm, ffn_out, norm_gains[3])
    ffn_grad, gain_three = pull_post(grad_rows)
    ffn_all = place.gather_tokens(ffn_grad.astype(low))
    down_part = dot(hidden, ffn_all, 0, 0).astype(low)
    hidden_grad = dot(ffn_all, down_mat, 1, 1)
    gate_low = (hidden_grad * gate_factor.astype(full)).astype(low)
    up_low = (hidden_grad * up_factor.astype(full)).astype(low)
    gate_part = dot(gate_low, normed_all, 0, 0).astype(low)
    up_part = dot(up_low, normed_all, 0, 0).astype(low)
    normed_ffn_grad = place.scatter_tokens(dot(gate_low, gate_mat, 1, 0) + dot(up_low, up_mat, 1, 0))

    down_sum = place.scatter_down(down_part.reshape(-1, unit, width))
    gate_up_sum = place.sum_pairs(
        place.scatter_chips(jnp.concatenate([gate_part, up_part], 0).reshape(-1, unit, width))
    )
    other = place.swap_rep(gate_up_sum)
    gate_up_sum = jnp.where(
        par == 0, jnp.stack([gate_up_sum, other]), jnp.stack([other, gate_up_sum])
    ).reshape(2 * unit, width)

    unused, pull_pre = jax.vjp(rms_norm, middle, norm_gains[2])
    middle_part, gain_two = pull_pre(normed_ffn_grad)
    middle_grad = grad_rows + middle_part
    unused, pull_attn = jax.vjp(rms_norm, attn_out, norm_gains[1])
    attn_grad, gain_one = pull_attn(middle_grad)
    attn_low = attn_grad.astype(low)
    out_part = dot(context, attn_low, 0, 0)
    context_grad = dot(attn_low, out_mat, 1, 1).astype(low).reshape(groups, length, -1)
    head_grads = jax.vmap(attend_back)(context_grad, probs, query_low, key_low, value_low)
    unused, pull_heads = jax.vjp(
        lambda rows, gains: jax.vmap(split_heads, (0, None, 0, 0))(rows, gains, cosine, sine_part),
        qkv,
        head_gains,
    )
    qkv_grad, head_grad = pull_heads(head_grads)
    qkv_low = qkv_grad.astype(low).reshape(groups * length, -1)
    qkv_part = dot(qkv_low, normed, 0, 0)
    normed_grad = dot(qkv_low, qkv_mat, 1, 0)
    unused, pull_first = jax.vjp(rms_norm, block_in, norm_gains[0])
    first_part, gain_zero = pull_first(normed_grad)
    input_grad = (middle_grad + first_part).reshape(tokens.shape)

    norm_grad = jnp.stack([gain_zero, gain_one, gain_two, gain_three])
    norm_w, head_w = width // place.shards, HD // place.shards
    gains = jnp.concatenate(
        [
            norm_grad.reshape(4, place.shards, norm_w).transpose(1, 0, 2).reshape(place.shards, -1),
            head_grad.reshape(2, place.shards, head_w).transpose(1, 0, 2).reshape(place.shards, -1),
        ],
        1,
    )
    gains = jnp.pad(gains[:, None, :], ((0, 0), (0, PAD - 1), (0, width - gains.shape[1])))
    attn_part = jnp.concatenate(
        [qkv_part.reshape(place.shards, qw, width), out_part.reshape(place.shards, ow, width), gains], 1
    ).astype(low)
    attn_part = attn_part.reshape((place.chips, 2) + attn_part.shape[1:])
    away = lax.dynamic_index_in_dim(attn_part, 1 - core, 1, keepdims=False)
    mine = lax.dynamic_index_in_dim(attn_part, core, 1, keepdims=False)
    attn_part = (mine.astype(full) + place.swap_core(away).astype(full)).astype(low)
    attn_sum = place.sum_pairs(place.scatter_chips(attn_part))
    attn_sum = attn_sum.astype(full) + place.swap_rep(attn_sum).astype(full)
    qkv_sum = attn_sum[:qw].T
    out_sum = attn_sum[qw : qw + ow]
    gains = attn_sum[qw + ow]
    norm_gain_grad = gains[: 4 * norm_w].reshape(4, norm_w)
    head_gain_grad = gains[4 * norm_w : 4 * norm_w + 2 * head_w].reshape(2, head_w)
    gate_up_grad = gate_up_sum.astype(full).T
    down_grad = down_sum.astype(full)

    total_tokens = groups * length * place.reps * place.shards
    scale = float(total_tokens) ** (-0.5)
    fresh, new_stats = [], []
    for at, (grad, weight, by_column) in enumerate(
        (
            (qkv_sum, qkv_weight, True),
            (out_sum, out_weight, False),
            (gate_up_grad, gate_up_weight, True),
            (down_grad, down_weight, False),
        )
    ):
        left, right, left_root, right_root = stats[4 * at : 4 * at + 4]
        cut = column_blocks if by_column else row_blocks
        sizes = (left.shape[-1], right.shape[-1])
        blocks, new_left, new_right = refresh(
            cut(grad * scale, *sizes), cut(weight, *sizes), left, right, left_root, right_root, decay[at], rate[at]
        )
        fresh.append(column_full(blocks) if by_column else row_full(blocks))
        new_stats += [new_left, new_right]
    return (
        block_output,
        input_grad,
        norm_gain_grad,
        head_gain_grad,
        qkv_sum,
        out_sum,
        gate_up_grad,
        down_grad,
        *fresh,
        *new_stats,
    )


def solution(mesh):
    place = Place(mesh)
    tokens3, rows2 = P(AXES, None, None), P("shard", None)
    columns2, blocks4 = P(None, "shard"), P("shard", None, None, None)

    def run(*args):
        return per_device(place, *args)

    return jax.shard_map(
        run,
        mesh=mesh,
        in_specs=(tokens3, tokens3, P(AXES, None), P(), P(), columns2, rows2, columns2, rows2)
        + (blocks4,) * 16
        + (P(), P()),
        out_specs=(tokens3, tokens3, columns2, columns2, columns2, rows2, columns2, rows2)
        + (columns2, rows2, columns2, rows2)
        + (blocks4,) * 8,
        check_vma=False,
    )
```

time: 1470 us -> 883 us (0.60)
  waiting for transfers between devices: 836 us -> 251 us
  matrix products: 405 us -> 230 us
  starting transfers between devices: 1.03 us -> 134 us
  local copies, waits for them, and re-layouts: 72.3 us -> 137 us
  blocking collectives: 38.4 us -> 0 us
  other arithmetic: 86.2 us -> 115 us
    reduce_scatter x4 -> x0, waiting for transfers between devices: 502 us -> none  [the longest x1 324 us: per_device(): lax.psum_scatter(gate_up_part.astype(jnp.bfloat16), 'shard', scatter_dime...]
    all_gather x4 -> x0, waiting for transfers between devices: 260 us -> none  [the longest x1 153 us: fetch_ffn(): lax.all_gather(gate_up_weight.astype(jnp.bfloat16), 'shard', axis=1, tile...]
    ppermute x0 -> x57, waiting for transfers between devices: none -> 251 us  [send(): return lax.ppermute(value, AXES, pairs)]
    dot_general x52 -> x32, matrix products: 405 us -> 226 us  [the longest x15 161 us: dot(): lax.dot_general(a, b, (((ca,), (cb,)), ((), ())), preferred_element_type=...]
    ppermute x0 -> x57, starting transfers between devices: none -> 134 us  [send(): return lax.ppermute(value, AXES, pairs)]
    psum x1 -> x0, waiting for transfers between devices: 73.5 us -> none  [per_device(): lax.psum(qkv_owned.astype(jnp.bfloat16), 'rep').astype(jnp.float32)]
    unnamed x1 -> x0, blocking collectives: 33.3 us -> none
    convert_element_type x0 -> x9, local copies, waits for them, and re-layouts: none -> 21.8 us  [the longest x8 19.3 us: mul(): b.astype(low)]
  transfers between devices with their start and end apart: 10 -> 57, of which waited for: 8 -> 25; matrix products, arithmetic and copies ran while one was open for 19% -> 35% of each run, Pallas kernels for 0% -> 0%
where the time goes in v1:
time: 883 us; the launch traced here: 873 us
  waiting for transfers between devices  251 us (28%)
  matrix products  230 us (26%)
  local copies, waits for them, and re-layouts  137 us (16%)
  starting transfers between devices  134 us (15%)
  other arithmetic  115 us (13%)
    ppermute x57, waiting for transfers between devices, send(): return lax.ppermute(value, AXES, pairs)  251 us
    dot_general x15, matrix products, dot(): lax.dot_general(a, b, (((ca,), (cb,)), ((), ())), preferred_element_type=...  161 us
    ppermute x57, starting transfers between devices, send(): return lax.ppermute(value, AXES, pairs)  134 us
    dot_general x12, matrix products, mul(): jnp.einsum(spec, a.astype(low), b.astype(low), preferred_element_type=full)  57.5 us
    unnamed x256, local copies, waits for them, and re-layouts  45.9 us
    convert_element_type x8, local copies, waits for them, and re-layouts, mul(): b.astype(low)  19.3 us
    convert_element_type x9, other arithmetic, scatter_line(): mine = (mine.astype(full) + got.astype(full)).astype(low)  18 us
  transfers between devices with their start and end apart: 57, of which 25 were waited for; matrix products, arithmetic and copies ran while one was open for 35% of the time, Pallas kernels for 0%

profile of v1, /device:TPU:0, one launch (start us, length us, event | category | flops | bytes accessed | tf_op | source)
XLA Modules:
  0.0 873.5 jit_solution(1658883131154379248)
XLA Ops:
  6.7 5.9 collective-permute-start.10
  25.0 16.2 %collective-permute-done = bf16[160,1152]{1,0:T(8,128)(2,1)} collective-permute-done((bf16[160,1152]{1,0:T(8,128)(2,1)}, bf16[160,1152]{1,0:T(8,128)(2,1)}, u32[]{:S(2)}, u32[]{:S(2)}) %collective-permute-start) | collective-permute-done | bytes 368672 | tf_op jit(solution)/shard_map/ppermute | solution.py:45
  78.3 7.2 collective-permute-done.11
  90.5 28.3 %collective-permute-done.14 = bf16[432,1152]{1,0:T(8,128)(2,1)S(1)} collective-permute-done((bf16[432,1152]{1,0:T(8,128)(2,1)}, bf16[432,1152]{1,0:T(8,128)(2,1)S(1)}, u32[]{:S(2)}, u32[]{:S(2)}) %collective-permute-start.14) | collective-permute-done | bytes 995360 | tf_op jit(solution)/shard_map/ppermute | solution.py:45
  128.9 7.5 collective-permute-done.19
  223.3 12.6 %collective-permute-done.16 = bf16[4,432,1152]{2,1,0:T(8,128)(2,1)} collective-permute-done((bf16[4,432,1152]{2,1,0:T(8,128)(2,1)}, bf16[4,432,1152]{2,1,0:T(8,128)(2,1)}, u32[]{:S(2)}, u32[]{:S(2)}) %collective-permute-start.16) | collective-permute-done | bytes 3981344 | tf_op jit(solution)/shard_map/ppermute | solution.py:45
  243.3 24.4 %collective-permute-done.24 = bf16[4,432,1152]{2,1,0:T(8,128)(2,1)} collective-permute-done((bf16[4,432,1152]{2,1,0:T(8,128)(2,1)}, bf16[4,432,1152]{2,1,0:T(8,128)(2,1)}, u32[]{:S(2)}, u32[]{:S(2)}) %collective-permute-start.24) | collective-permute-done | bytes 3981344 | tf_op jit(solution)/shard_map/ppermute | solution.py:45
  270.1 14.1 %fusion.146 = f32[2048,1728]{0,1:T(8,128)} fusion(bf16[1728,1152]{1,0:T(8,128)(2,1)S(1)} %bitcast.399, bf16[1024,1152]{1,0:T(8,128)(2,1)S(1)} %collective-permute-done.9, bf16[512,1152]{1,0:T(8,128)(2,1)} %collective-permute-done.8, bf16[512,1152]{1,0:T(8,128)(2,1)S(1)} %multiply_convert_fusion.4), kind=kOutput, calls=%fused_computation.328 | convolution fusion | flops 8167882752 | bytes 22855680 | tf_op jit(solution)/shard_map/dot_general | solution.py:20
  284.2 22.0 %multiply_convert_fusion.2 = (bf16[2048,1728]{0,1:T(8,128)(2,1)}, f32[2048,1728]{0,1:T(8,128)}) fusion(f32[2048,1728]{0,1:T(8,128)} %fusion.146, bf16[1728,1152]{1,0:T(8,128)(2,1)} %bitcast.397, bf16[1024,1152]{1,0:T(8,128)(2,1)} %copy-done.107, bf16[512,1152]{1,0:T(8,128)(2,1)} %collective-permute-done.8, bf16[512,1152]{1,0:T(8,128)(2,1)S(1)} %multiply_convert_fusion.4), kind=kOutput, calls=%fused_computation.14 | convolution fusion | flops 8203272192 | bytes 44089344 | tf_op jit(solution)/shard_map/dot_general | solution.py:20
  306.2 13.9 %fusion.153 = f32[2048,1152]{1,0:T(8,128)S(1)} fusion(bf16[2048,1728]{0,1:T(8,128)(2,1)} %get-tuple-element.197, bf16[1728,1152]{1,0:T(8,128)(2,1)} %bitcast.395), kind=kOutput, calls=%fused_computation.335 | convolution fusion | flops 8153726976 | bytes 20496384 | tf_op jit(solution)/shard_map/dot_general | solution.py:20
  329.4 26.7 %collective-permute-done.26 = bf16[512,1152]{1,0:T(8,128)(2,1)S(1)} collective-permute-done((bf16[512,1152]{1,0:T(8,128)(2,1)S(1)}, bf16[512,1152]{1,0:T(8,128)(2,1)S(1)}, u32[]{:S(2)}, u32[]{:S(2)}) %collective-permute-start.26) | collective-permute-done | bytes 1179680 | tf_op jit(solution)/shard_map/ppermute | solution.py:45
  361.2 25.9 %collective-permute-done.27 = bf16[512,1152]{1,0:T(8,128)(2,1)S(1)} collective-permute-done((bf16[512,1152]{1,0:T(8,128)(2,1)S(1)}, bf16[512,1152]{1,0:T(8,128)(2,1)S(1)}, u32[]{:S(2)}, u32[]{:S(2)}) %collective-permute-start.27) | collective-permute-done | bytes 1179680 | tf_op jit(solution)/shard_map/ppermute | solution.py:45
  394.7 26.9 %multiply_convert_fusion = (bf16[2048,1728]{0,1:T(8,128)(2,1)}, bf16[2048,1728]{0,1:T(8,128)(2,1)}) fusion(f32[2048,1728]{0,1:T(8,128)} %fusion.146, f32[2048,1728]{0,1:T(8,128)} %get-tuple-element.198, bf16[1728,1152]{1,0:T(8,128)(2,1)} %bitcast.396, bf16[1024,1152]{1,0:T(8,128)(2,1)} %collective-permute-done.28, bf16[512,1152]{1,0:T(8,128)(2,1)} %copy-done.61, ...), kind=kOutput, calls=%fused_computation.12 | convolution fusion | flops 8263434240 | bytes 51167232 | tf_op jit(solution)/shard_map/dot_general | solution.py:20
  421.6 14.5 %fusion.154 = f32[2048,1152]{1,0:T(8,128)} fusion(bf16[2048,1728]{0,1:T(8,128)(2,1)} %get-tuple-element.150, bf16[1728,1152]{1,0:T(8,128)(2,1)S(1)} %bitcast.400), kind=kOutput, calls=%fused_computation.336 | convolution fusion | flops 8153726976 | bytes 20496384 | tf_op jit(solution)/shard_map/dot_general | solution.py:20
  436.1 14.2 %convolution_add_fusion = f32[2048,1152]{1,0:T(8,128)S(1)} fusion(f32[2048,1152]{1,0:T(8,128)} %fusion.154, bf16[2048,1728]{0,1:T(8,128)(2,1)} %get-tuple-element.149, bf16[1728,1152]{1,0:T(8,128)(2,1)S(1)} %bitcast.398), kind=kOutput, calls=%fused_computation.21 | convolution fusion | flops 8156086272 | bytes 29933568 | tf_op jit(solution)/shard_map/dot_general | solution.py:20
  451.9 13.6 %convolution_convert_fusion = bf16[1728,1152]{1,0:T(8,128)(2,1)} fusion(bf16[2048,1728]{0,1:T(8,128)(2,1)} %get-tuple-element.197, bf16[1024,1152]{1,0:T(8,128)(2,1)} %collective-permute-done.28, bf16[512,1152]{1,0:T(8,128)(2,1)S(1)} %copy-done.62, bf16[512,1152]{1,0:T(8,128)(2,1)S(1)} %copy-done.27), kind=kOutput, calls=%fused_computation.29 | convolution fusion | flops 8169873408 | bytes 15777792 | tf_op jit(solution)/shard_map/dot_general | solution.py:20
  466.9 13.3 %convolution_convert_fusion.1 = bf16[1728,1152]{1,0:T(8,128)(2,1)} fusion(bf16[2048,1728]{0,1:T(8,128)(2,1)} %get-tuple-element.149, bf16[1024,1152]{1,0:T(8,128)(2,1)S(1)} %copy-done.108, bf16[512,1152]{1,0:T(8,128)(2,1)} %collective-permute-done.8, bf16[512,1152]{1,0:T(8,128)(2,1)S(1)} %copy-done.29), kind=kOutput, calls=%fused_computation.30 | convolution fusion | flops 8169873408 | bytes 15777792 | tf_op jit(solution)/shard_map/dot_general | solution.py:20
  480.2 13.1 %convolution_convert_fusion.2 = bf16[1728,1152]{1,0:T(8,128)(2,1)} fusion(bf16[2048,1728]{0,1:T(8,128)(2,1)} %get-tuple-element.150, bf16[1024,1152]{1,0:T(8,128)(2,1)S(1)} %copy-done.108, bf16[512,1152]{1,0:T(8,128)(2,1)} %collective-permute-done.8, bf16[512,1152]{1,0:T(8,128)(2,1)S(1)} %copy-done.29), kind=kOutput, calls=%fused_computation.31 | convolution fusion | flops 8169873408 | bytes 15777792 | tf_op jit(solution)/shard_map/dot_general | solution.py:20
  498.5 7.2 pad_maximum_fusion.4
  514.9 8.0 collective-permute-done.30
  569.8 6.9 add_convert_fusion
  576.7 25.1 %collective-permute-done.40 = bf16[4,432,1152]{2,1,0:T(8,128)(2,1)} collective-permute-done((bf16[4,432,1152]{2,1,0:T(8,128)(2,1)}, bf16[4,432,1152]{2,1,0:T(8,128)(2,1)}, u32[]{:S(2)}, u32[]{:S(2)}) %collective-permute-start.40) | collective-permute-done | bytes 3981344 | tf_op jit(solution)/shard_map/ppermute | solution.py:45
  608.8 6.2 pad_maximum_fusion
  629.3 12.0 %collective-permute-done.41 = bf16[432,1152]{1,0:T(8,128)(2,1)} collective-permute-done((bf16[432,1152]{1,0:T(8,128)(2,1)}, bf16[432,1152]{1,0:T(8,128)(2,1)}, u32[]{:S(2)}, u32[]{:S(2)}) %collective-permute-start.41) | collective-permute-done | bytes 995360 | tf_op jit(solution)/shard_map/ppermute | solution.py:45
  666.1 6.2 reshape.522
  708.7 11.4 %collective-permute-done.53 = bf16[432,1152]{1,0:T(8,128)(2,1)S(1)} collective-permute-done((bf16[432,1152]{1,0:T(8,128)(2,1)S(1)}, bf16[432,1152]{1,0:T(8,128)(2,1)S(1)}, u32[]{:S(2)}, u32[]{:S(2)}) %collective-permute-start.53) | collective-permute-done | bytes 995360 | tf_op jit(solution)/shard_map/ppermute | solution.py:45
  722.8 7.9 collective-permute-done.46
  739.3 6.4 collective-permute-done.54
  770.6 5.8 copy.299
  776.4 14.3 %multiply_add_fusion.1 = f32[2,9,432,432]{3,2,1,0:T(8,128)} fusion(f32[2,9,432,432]{3,2,1,0:T(8,128)} %param.45, f32[]{:T(128)S(6)} %sub.153, f32[]{:T(128)} %bitcast.126, bf16[2,9,128,432]{2,3,1,0:T(8,128)(2,1)S(1)} %copy.299), kind=kOutput, calls=%fused_computation.3 | convolution fusion | flops 870041088 | bytes 28864520 | tf_op jit(solution)/shard_map/sbji,sbjk->sbik/dot_general | solution.py:272
  790.7 14.5 %bitcast_subtract_fusion = f32[9,128,2,432]{1,3,0,2:T(8,128)} fusion(f32[9,128,2,432]{1,0,3,2:T(8,128)} %reshape.522, f32[2,9,432,432]{3,2,1,0:T(8,128)} %param.47, bf16[2,9,128,432]{2,3,1,0:T(8,128)(2,1)S(1)} %copy.299, f32[]{:T(128)} %bitcast.117, f32[2,9,128,128]{3,2,1,0:T(8,128)} %param.46), kind=kOutput, calls=%fused_computation.45 | convolution fusion | flops 1121407488 | bytes 24569860 | tf_op jit(solution)/shard_map/sbij,sbjk->sbik/dot_general | solution.py:272
  818.0 6.9 bitcast_subtract_fusion.2
  (535 shorter events, 428.8 us)
Async XLA Ops:
  6.7 55.0 %collective-permute-start.10 = (bf16[432,1152]{1,0:T(8,128)(2,1)}, bf16[432,1152]{1,0:T(8,128)(2,1)}, u32[]{:S(2)}, u32[]{:S(2)}) collective-permute-start(bf16[432,1152]{1,0:T(8,128)(2,1)} %dynamic-slice_bitcast_fusion.7), channel_id=1, source_target_pairs={{0,4},{1,5},{2,6},{3,7},{4,8},{5,9},{6,10},{7,11},{8,12},{9,13},{1... | collective-permute-start | bytes 2985992 | tf_op jit(solution)/shard_map/ppermute | solution.py:45
  12.6 64.0 %collective-permute-start.13 = (bf16[432,1152]{1,0:T(8,128)(2,1)}, bf16[432,1152]{1,0:T(8,128)(2,1)}, u32[]{:S(2)}, u32[]{:S(2)}) collective-permute-start(bf16[432,1152]{1,0:T(8,128)(2,1)} %dynamic-slice_bitcast_fusion.7), channel_id=1, source_target_pairs={{4,0},{5,1},{6,2},{7,3},{8,4},{9,5},{10,6},{11,7},{12,8},{13,9},{1... | collective-permute-start | bytes 2985992 | tf_op jit(solution)/shard_map/ppermute | solution.py:45
  20.7 28.4 %collective-permute-start.3 = (bf16[160,1152]{1,0:T(8,128)(2,1)}, bf16[160,1152]{1,0:T(8,128)(2,1)}, u32[]{:S(2)}, u32[]{:S(2)}) collective-permute-start(bf16[160,1152]{1,0:T(8,128)(2,1)} %pad_maximum_fusion.14), channel_id=1, source_target_pairs={{4,0},{5,1},{6,2},{7,3},{8,4},{9,5},{10,6},{11,7},{12,8},{13,9},{1... | collective-permute-start | bytes 1105928 | tf_op jit(solution)/shard_map/ppermute | solution.py:45
  23.1 49.2 %collective-permute-start.17 = (bf16[432,1152]{1,0:T(8,128)(2,1)}, bf16[432,1152]{1,0:T(8,128)(2,1)}, u32[]{:S(2)}, u32[]{:S(2)}) collective-permute-start(bf16[432,1152]{1,0:T(8,128)(2,1)} %convert_element_type.482), channel_id=1, source_target_pairs={{0,1},{1,0},{2,3},{3,2},{4,5},{5,4},{6,7},{7,6},{8,9},{9,8},{10,11... | collective-permute-start | bytes 2985992 | tf_op jit(solution)/shard_map/ppermute | solution.py:45
  70.8 55.3 %collective-permute-start.6 = (bf16[4,160,1152]{2,1,0:T(8,128)(2,1)S(1)}, bf16[4,160,1152]{2,1,0:T(8,128)(2,1)S(1)}, u32[]{:S(2)}, u32[]{:S(2)}) collective-permute-start(bf16[4,160,1152]{2,1,0:T(8,128)(2,1)S(1)} %constant_dynamic-slice_fusion.2), channel_id=1, source_target_pairs={{0,2},{1,3},{2,0},{3,1},{4,6},{5,7},{6,4},{7,5},{8,10},{9,11},{10,... | collective-permute-start | bytes 4423688 | tf_op jit(solution)/shard_map/ppermute | solution.py:45
  72.5 47.6 %collective-permute-start.18 = (bf16[432,1152]{1,0:T(8,128)(2,1)S(1)}, bf16[432,1152]{1,0:T(8,128)(2,1)S(1)}, u32[]{:S(2)}, u32[]{:S(2)}) collective-permute-start(bf16[432,1152]{1,0:T(8,128)(2,1)S(1)} %broadcast_select_fusion.1), channel_id=1, source_target_pairs={{0,4},{3,7},{4,8},{7,11},{8,12},{11,15},{16,20},{19,23},{20,24},{2... | collective-permute-start | bytes 2985992 | tf_op jit(solution)/shard_map/ppermute | solution.py:45
  75.3 49.4 %collective-permute-start.21 = (bf16[432,1152]{1,0:T(8,128)(2,1)S(1)}, bf16[432,1152]{1,0:T(8,128)(2,1)S(1)}, u32[]{:S(2)}, u32[]{:S(2)}) collective-permute-start(bf16[432,1152]{1,0:T(8,128)(2,1)S(1)} %broadcast_select_fusion.1), channel_id=1, source_target_pairs={{4,0},{7,3},{8,4},{11,7},{12,8},{15,11},{20,16},{23,19},{24,20},{2... | collective-permute-start | bytes 2985992 | tf_op jit(solution)/shard_map/ppermute | solution.py:45
  76.6 42.2 %collective-permute-start.14 = (bf16[432,1152]{1,0:T(8,128)(2,1)}, bf16[432,1152]{1,0:T(8,128)(2,1)S(1)}, u32[]{:S(2)}, u32[]{:S(2)}) collective-permute-start(bf16[432,1152]{1,0:T(8,128)(2,1)} %collective-permute-done.13), channel_id=1, source_target_pairs={{4,0},{5,1},{6,2},{7,3},{8,4},{9,5},{10,6},{11,7},{12,8},{13,9},{1... | collective-permute-start | bytes 2985992 | tf_op jit(solution)/shard_map/ppermute | solution.py:45
  85.5 41.3 %collective-permute-start.12 = (bf16[432,1152]{1,0:T(8,128)(2,1)S(1)}, bf16[432,1152]{1,0:T(8,128)(2,1)S(1)}, u32[]{:S(2)}, u32[]{:S(2)}) collective-permute-start(bf16[432,1152]{1,0:T(8,128)(2,1)S(1)} %collective-permute-done.11), channel_id=1, source_target_pairs={{0,4},{1,5},{2,6},{3,7},{4,8},{5,9},{6,10},{7,11},{8,12},{9,13},{1... | collective-permute-start | bytes 2985992 | tf_op jit(solution)/shard_map/ppermute | solution.py:45
  146.6 89.3 %collective-permute-start.16 = (bf16[4,432,1152]{2,1,0:T(8,128)(2,1)}, bf16[4,432,1152]{2,1,0:T(8,128)(2,1)}, u32[]{:S(2)}, u32[]{:S(2)}) collective-permute-start(bf16[4,432,1152]{2,1,0:T(8,128)(2,1)} %constant_dynamic-slice_fusion.1), channel_id=1, source_target_pairs={{0,2},{1,3},{2,0},{3,1},{4,6},{5,7},{6,4},{7,5},{8,10},{9,11},{10,... | collective-permute-start | bytes 11943944 | tf_op jit(solution)/shard_map/ppermute | solution.py:45
  146.6 58.9 %collective-permute-start.23 = (bf16[432,1152]{1,0:T(8,128)(2,1)}, bf16[432,1152]{1,0:T(8,128)(2,1)}, u32[]{:S(2)}, u32[]{:S(2)}) collective-permute-start(bf16[432,1152]{1,0:T(8,128)(2,1)} %collective-permute-done.22), channel_id=1, source_target_pairs={{4,0},{7,3},{8,4},{11,7},{12,8},{15,11},{20,16},{23,19},{24,20},{2... | collective-permute-start | bytes 2985992 | tf_op jit(solution)/shard_map/ppermute | solution.py:45
  212.3 55.5 %collective-permute-start.24 = (bf16[4,432,1152]{2,1,0:T(8,128)(2,1)}, bf16[4,432,1152]{2,1,0:T(8,128)(2,1)}, u32[]{:S(2)}, u32[]{:S(2)}) collective-permute-start(bf16[4,432,1152]{2,1,0:T(8,128)(2,1)} %constant_dynamic-slice_fusion), channel_id=1, source_target_pairs={{0,2},{3,1},{4,6},{7,5},{8,10},{11,9},{12,14},{15,13},{16,18},{19,... | collective-permute-start | bytes 11943944 | tf_op jit(solution)/shard_map/ppermute | solution.py:45
  223.2 46.9 %collective-permute-start.9 = (bf16[1024,1152]{1,0:T(8,128)(2,1)S(1)}, bf16[1024,1152]{1,0:T(8,128)(2,1)S(1)}, u32[]{:S(2)}, u32[]{:S(2)}) collective-permute-start(bf16[1024,1152]{1,0:T(8,128)(2,1)S(1)} %pad_maximum_fusion.9), channel_id=1, source_target_pairs={{0,1},{1,0},{2,3},{3,2},{4,5},{5,4},{6,7},{7,6},{8,9},{9,8},{10,11... | collective-permute-start | bytes 7077896 | tf_op jit(solution)/shard_map/ppermute | solution.py:45
  450.6 42.7 %collective-permute-start.29 = (bf16[1024,1152]{1,0:T(8,128)(2,1)S(1)}, bf16[1024,1152]{1,0:T(8,128)(2,1)S(1)}, u32[]{:S(2)}, u32[]{:S(2)}) collective-permute-start(bf16[1024,1152]{1,0:T(8,128)(2,1)S(1)} %slice.240), channel_id=1, source_target_pairs={{0,1},{1,0},{2,3},{3,2},{4,5},{5,4},{6,7},{7,6},{8,9},{9,8},{10,11... | collective-permute-start | bytes 7077896 | tf_op jit(solution)/shard_map/ppermute | solution.py:45
  465.6 104.3 %collective-permute-start.48 = (bf16[4,432,1152]{2,1,0:T(8,128)(2,1)}, bf16[4,432,1152]{2,1,0:T(8,128)(2,1)}, u32[]{:S(2)}, u32[]{:S(2)}) collective-permute-start(bf16[4,432,1152]{2,1,0:T(8,128)(2,1)} %bitcast.103), channel_id=1, source_target_pairs={{1,3},{2,0},{5,7},{6,4},{9,11},{10,8},{13,15},{14,12},{17,19},{18,... | collective-permute-start | bytes 11943944 | tf_op jit(solution)/shard_map/ppermute | solution.py:45
  510.3 91.5 %collective-permute-start.40 = (bf16[4,432,1152]{2,1,0:T(8,128)(2,1)}, bf16[4,432,1152]{2,1,0:T(8,128)(2,1)}, u32[]{:S(2)}, u32[]{:S(2)}) collective-permute-start(bf16[4,432,1152]{2,1,0:T(8,128)(2,1)} %dynamic-slice_bitcast_fusion), channel_id=1, source_target_pairs={{0,2},{1,3},{2,0},{3,1},{4,6},{5,7},{6,4},{7,5},{8,10},{9,11},{10,... | collective-permute-start | bytes 11943944 | tf_op jit(solution)/shard_map/ppermute | solution.py:45
  623.9 69.0 %collective-permute-start.31 = (bf16[8,176,1152]{2,1,0:T(8,128)(2,1)}, bf16[8,176,1152]{2,1,0:T(8,128)(2,1)}, u32[]{:S(2)}, u32[]{:S(2)}) collective-permute-start(bf16[8,176,1152]{2,1,0:T(8,128)(2,1)} %dynamic-slice_bitcast_fusion.1), channel_id=1, source_target_pairs={{0,1},{1,0},{2,3},{3,2},{4,5},{5,4},{6,7},{7,6},{8,9},{9,8},{10,11... | collective-permute-start | bytes 9732104 | tf_op jit(solution)/shard_map/ppermute | solution.py:45
  625.0 30.5 %collective-permute-start.49 = (bf16[432,1152]{1,0:T(8,128)(2,1)S(1)}, bf16[432,1152]{1,0:T(8,128)(2,1)}, u32[]{:S(2)}, u32[]{:S(2)}) collective-permute-start(bf16[432,1152]{1,0:T(8,128)(2,1)S(1)} %get-tuple-element.153), channel_id=1, source_target_pairs={{0,4},{3,7},{4,8},{7,11},{8,12},{11,15},{16,20},{19,23},{20,24},{2... | collective-permute-start | bytes 2985992 | tf_op jit(solution)/shard_map/ppermute | solution.py:45
  627.8 51.3 %collective-permute-start.44 = (bf16[432,1152]{1,0:T(8,128)(2,1)}, bf16[432,1152]{1,0:T(8,128)(2,1)}, u32[]{:S(2)}, u32[]{:S(2)}) collective-permute-start(bf16[432,1152]{1,0:T(8,128)(2,1)} %get-tuple-element.158), channel_id=1, source_target_pairs={{4,0},{5,1},{6,2},{7,3},{8,4},{9,5},{10,6},{11,7},{12,8},{13,9},{1... | collective-permute-start | bytes 2985992 | tf_op jit(solution)/shard_map/ppermute | solution.py:45
  643.9 35.3 %collective-permute-start.42 = (bf16[432,1152]{1,0:T(8,128)(2,1)}, bf16[432,1152]{1,0:T(8,128)(2,1)}, u32[]{:S(2)}, u32[]{:S(2)}) collective-permute-start(bf16[432,1152]{1,0:T(8,128)(2,1)} %fusion.39), channel_id=1, source_target_pairs={{0,4},{1,5},{2,6},{3,7},{4,8},{5,9},{6,10},{7,11},{8,12},{9,13},{1... | collective-permute-start | bytes 2985992 | tf_op jit(solution)/shard_map/ppermute | solution.py:45
  649.4 38.4 %collective-permute-start.52 = (bf16[432,1152]{1,0:T(8,128)(2,1)}, bf16[432,1152]{1,0:T(8,128)(2,1)}, u32[]{:S(2)}, u32[]{:S(2)}) collective-permute-start(bf16[432,1152]{1,0:T(8,128)(2,1)} %get-tuple-element.154), channel_id=1, source_target_pairs={{4,0},{7,3},{8,4},{11,7},{12,8},{15,11},{20,16},{23,19},{24,20},{2... | collective-permute-start | bytes 2985992 | tf_op jit(solution)/shard_map/ppermute | solution.py:45
  658.2 30.8 %collective-permute-start.50 = (bf16[432,1152]{1,0:T(8,128)(2,1)}, bf16[432,1152]{1,0:T(8,128)(2,1)}, u32[]{:S(2)}, u32[]{:S(2)}) collective-permute-start(bf16[432,1152]{1,0:T(8,128)(2,1)} %fusion.33), channel_id=1, source_target_pairs={{0,4},{3,7},{4,8},{7,11},{8,12},{11,15},{16,20},{19,23},{20,24},{2... | collective-permute-start | bytes 2985992 | tf_op jit(solution)/shard_map/ppermute | solution.py:45
  683.2 39.6 %collective-permute-start.43 = (bf16[432,1152]{1,0:T(8,128)(2,1)S(1)}, bf16[432,1152]{1,0:T(8,128)(2,1)S(1)}, u32[]{:S(2)}, u32[]{:S(2)}) collective-permute-start(bf16[432,1152]{1,0:T(8,128)(2,1)S(1)} %get-tuple-element.155), channel_id=1, source_target_pairs={{0,4},{1,5},{2,6},{3,7},{4,8},{5,9},{6,10},{7,11},{8,12},{9,13},{1... | collective-permute-start | bytes 2985992 | tf_op jit(solution)/shard_map/ppermute | solution.py:45
  691.5 28.5 %collective-permute-start.53 = (bf16[432,1152]{1,0:T(8,128)(2,1)S(1)}, bf16[432,1152]{1,0:T(8,128)(2,1)S(1)}, u32[]{:S(2)}, u32[]{:S(2)}) collective-permute-start(bf16[432,1152]{1,0:T(8,128)(2,1)S(1)} %get-tuple-element.152), channel_id=1, source_target_pairs={{4,0},{7,3},{8,4},{11,7},{12,8},{15,11},{20,16},{23,19},{24,20},{2... | collective-permute-start | bytes 2985992 | tf_op jit(solution)/shard_map/ppermute | solution.py:45
  695.8 37.8 %collective-permute-start.32 = (bf16[4,176,1152]{2,1,0:T(8,128)(2,1)S(1)}, bf16[4,176,1152]{2,1,0:T(8,128)(2,1)S(1)}, u32[]{:S(2)}, u32[]{:S(2)}) collective-permute-start(bf16[4,176,1152]{2,1,0:T(8,128)(2,1)S(1)} %dynamic-slice_bitcast_fusion.2), channel_id=1, source_target_pairs={{0,2},{1,3},{2,0},{3,1},{4,6},{5,7},{6,4},{7,5},{8,10},{9,11},{10,... | collective-permute-start | bytes 4866056 | tf_op jit(solution)/shard_map/ppermute | solution.py:45
  700.8 30.0 %collective-permute-start.46 = (bf16[432,1152]{1,0:T(8,128)(2,1)S(1)}, bf16[432,1152]{1,0:T(8,128)(2,1)S(1)}, u32[]{:S(2)}, u32[]{:S(2)}) collective-permute-start(bf16[432,1152]{1,0:T(8,128)(2,1)S(1)} %fusion.38), channel_id=1, source_target_pairs={{4,0},{5,1},{6,2},{7,3},{8,4},{9,5},{10,6},{11,7},{12,8},{13,9},{1... | collective-permute-start | bytes 2985992 | tf_op jit(solution)/shard_map/ppermute | solution.py:45
  704.1 35.2 %collective-permute-start.51 = (bf16[432,1152]{1,0:T(8,128)(2,1)S(1)}, bf16[432,1152]{1,0:T(8,128)(2,1)S(1)}, u32[]{:S(2)}, u32[]{:S(2)}) collective-permute-start(bf16[432,1152]{1,0:T(8,128)(2,1)S(1)} %get-tuple-element.151), channel_id=1, source_target_pairs={{0,4},{3,7},{4,8},{7,11},{8,12},{11,15},{16,20},{19,23},{20,24},{2... | collective-permute-start | bytes 2985992 | tf_op jit(solution)/shard_map/ppermute | solution.py:45
  732.3 28.4 %collective-permute-start.47 = (bf16[432,1152]{1,0:T(8,128)(2,1)S(1)}, bf16[432,1152]{1,0:T(8,128)(2,1)S(1)}, u32[]{:S(2)}, u32[]{:S(2)}) collective-permute-start(bf16[432,1152]{1,0:T(8,128)(2,1)S(1)} %fusion.42), channel_id=1, source_target_pairs={{0,16},{1,17},{2,18},{3,19},{4,20},{5,21},{6,22},{7,23},{8,24},{9,... | collective-permute-start | bytes 2985992 | tf_op jit(solution)/shard_map/ppermute | solution.py:45
  747.4 57.8 %collective-permute-start.55 = (bf16[432,1152]{1,0:T(8,128)(2,1)S(1)}, bf16[432,1152]{1,0:T(8,128)(2,1)}, u32[]{:S(2)}, u32[]{:S(2)}) collective-permute-start(bf16[432,1152]{1,0:T(8,128)(2,1)S(1)} %fusion.36), channel_id=1, source_target_pairs={{0,16},{3,18},{4,20},{7,22},{8,24},{11,26},{12,28},{15,30},{16,1},... | collective-permute-start | bytes 2985992 | tf_op jit(solution)/shard_map/ppermute | solution.py:45
  751.5 53.7 %collective-permute-start.56 = (bf16[432,1152]{1,0:T(8,128)(2,1)S(1)}, bf16[432,1152]{1,0:T(8,128)(2,1)}, u32[]{:S(2)}, u32[]{:S(2)}) collective-permute-start(bf16[432,1152]{1,0:T(8,128)(2,1)S(1)} %fusion.36), channel_id=1, source_target_pairs={{3,2},{7,6},{11,10},{15,14},{16,17},{20,21},{24,25},{28,29}} | collective-permute-start | bytes 2985992 | tf_op jit(solution)/shard_map/ppermute | solution.py:45
  753.1 61.2 %collective-permute-start.36 = (bf16[176,1152]{1,0:T(8,128)(2,1)}, bf16[176,1152]{1,0:T(8,128)(2,1)}, u32[]{:S(2)}, u32[]{:S(2)}) collective-permute-start(bf16[176,1152]{1,0:T(8,128)(2,1)} %get-tuple-element.166), channel_id=1, source_target_pairs={{4,0},{5,1},{6,2},{7,3},{8,4},{9,5},{10,6},{11,7},{12,8},{13,9},{1... | collective-permute-start | bytes 1216520 | tf_op jit(solution)/shard_map/ppermute | solution.py:45
  755.4 58.8 %collective-permute-start.34 = (bf16[176,1152]{1,0:T(8,128)(2,1)}, bf16[176,1152]{1,0:T(8,128)(2,1)}, u32[]{:S(2)}, u32[]{:S(2)}) collective-permute-start(bf16[176,1152]{1,0:T(8,128)(2,1)} %fusion.78), channel_id=1, source_target_pairs={{0,4},{1,5},{2,6},{3,7},{4,8},{5,9},{6,10},{7,11},{8,12},{9,13},{1... | collective-permute-start | bytes 1216520 | tf_op jit(solution)/shard_map/ppermute | solution.py:45
  (141 other events, 1973.3 us)

commit v2 on v1

--- a/solution.py
+++ b/solution.py
@@ -3,12 +3,15 @@
 import jax
 import jax.numpy as jnp
 from jax import lax
+from jax.experimental import pallas as pl
+from jax.experimental.pallas import tpu as pltpu
 from jax.sharding import PartitionSpec as P
 
 HQ = 4
 HD = 256
 AXES = ("rep", "shard")
 PAD = 16
+MESH = pl.DeviceIdType.MESH
 
 epsilon = 1e-06
 rope_base = 1000000.0
@@ -27,6 +30,7 @@
         self.chips = self.shards // 2
         self.outer = min(4, self.chips)
         self.inner = self.chips // self.outer
+        self.direct = self.reps == 2 and self.inner == 2
 
     def here(self):
         r, i = lax.axis_index("rep"), lax.axis_index("shard")
@@ -170,6 +174,211 @@
         return two[:quarter] + self.swap_rep(two[quarter:].astype(low)).astype(full)
 
 
+class Net:
+    def __init__(self, line):
+        self.line = line
+        r, i = lax.axis_index("rep"), lax.axis_index("shard")
+        z, x, c = i // 4, i // 2 % 2, i % 2
+        self.r, self.z, self.x, self.c = r, z, x, c
+
+        def at(r, z, x, c):
+            return (r, (z * 2 + x) * 2 + c)
+
+        self.up, self.down = at(r, z + 1, x, c), at(r, z - 1, x, c)
+        self.across, self.mate, self.diagonal = at(r, z, 1 - x, c), at(r, z, x, 1 - c), at(r, z, 1 - x, 1 - c)
+        self.twin, self.twin_mate = at(1 - r, z, x, c), at(1 - r, z, x, 1 - c)
+        self.has_up, self.has_down = z < line - 1, z > 0
+
+    def greet(self, others):
+        barrier = pltpu.get_barrier_semaphore()
+
+        def signal(to):
+            pl.semaphore_signal(barrier, inc=1, device_id=to, device_id_type=MESH)
+
+        pl.when(self.has_up)(lambda: signal(self.up))
+        pl.when(self.has_down)(lambda: signal(self.down))
+        for to in others:
+            signal(to)
+        both = self.has_up & self.has_down
+        pl.when(both)(lambda: pl.semaphore_wait(barrier, len(others) + 2))
+        pl.when(jnp.logical_not(both))(lambda: pl.semaphore_wait(barrier, len(others) + 1))
+
+
+def put(source, target, send, recv, to):
+    return pltpu.make_async_remote_copy(
+        src_ref=source, dst_ref=target, send_sem=send, recv_sem=recv, device_id=to, device_id_type=MESH
+    )
+
+
+def gather_weights(place, attn_own, gate_up_own, down_own, qw):
+    line, width, unit = place.outer, attn_own.shape[1], down_own.shape[0]
+    ow = attn_own.shape[0] - qw
+    cut = (unit // 2 + 15) // 16 * 16
+
+    def kernel(attn, gate_up, down, q_all, o_all, g_all, d_all, ts, tr, gs, gr, ds, dr, ls):
+        net = Net(line)
+        r, z, x, c = net.r, net.z, net.x, net.c
+        home, mine = c == x, c == r
+
+        def attn_refs(zz, xx, cc):
+            i = (zz * 2 + xx) * 2 + cc
+            return [q_all.at[pl.ds(i * qw, qw)], o_all.at[pl.ds(i * ow, ow)]]
+
+        def ways(zz):
+            return ((0, net.has_up & (zz <= z), net.up), (1, net.has_down & (zz >= z), net.down))
+
+        def attn_fan(zz, act, own=False):
+            for part, ref in enumerate(attn_refs(zz, x, c)):
+                source = attn.at[pl.ds(part * qw, (qw, ow)[part])] if own else ref
+                for kind, when, to in ways(zz):
+                    pl.when(when)(lambda: act(put(source, ref, ts.at[kind, zz, part], tr.at[0, zz, part], to)))
+                act(put(source, ref, ts.at[2, zz, part], tr.at[1, zz, part], net.across))
+                act(put(source, ref, ts.at[3, zz, part], tr.at[2, zz, part], net.mate))
+
+        def attn_pass(zz, act):
+            for part, ref in enumerate(attn_refs(zz, 1 - x, c)):
+                act(put(ref, ref, ts.at[4, zz, part], tr.at[3, zz, part], net.mate))
+
+        def attn_wait(zz, kind):
+            xx, cc = (x, 1 - x, x, 1 - x)[kind], (c, c, 1 - c, 1 - c)[kind]
+            for part, ref in enumerate(attn_refs(zz, xx, cc)):
+                put(ref, ref, ts.at[0, zz, part], tr.at[kind, zz, part], net.mate).wait_recv()
+
+        def gate_fan(zz, act, own=False):
+            ref = g_all.at[zz * 2 + x]
+            source = gate_up if own else ref
+            for kind, when, to in ways(zz):
+                pl.when(when)(lambda: act(put(source, ref, gs.at[kind, zz], gr.at[0, zz], to)))
+            act(put(source, ref, gs.at[2, zz], gr.at[1, zz], net.across))
+
+        def gate_wait(zz, kind):
+            ref = g_all.at[zz * 2 + (x, 1 - x)[kind]]
+            put(ref, ref, gs.at[0, zz], gr.at[kind, zz], net.mate).wait_recv()
+
+        def down_refs(zz):
+            return [d_all.at[zz, pl.ds(0, cut)], d_all.at[zz, pl.ds(cut, unit - cut)]]
+
+        def down_first(act):
+            first, second = down_refs(z)
+            source = [down.at[pl.ds(0, cut)], down.at[pl.ds(cut, unit - cut)]]
+
+            @pl.when(jnp.logical_not(home))
+            def _():
+                act(put(source[0], first, ds.at[3, 0, 0], dr.at[0, z, 0], net.mate))
+                act(put(source[1], second, ds.at[3, 0, 1], dr.at[0, z, 1], net.mate))
+                act(put(source[1], second, ds.at[3, 1, 1], dr.at[0, z, 1], net.diagonal))
+
+            @pl.when(home)
+            def _():
+                act(put(source[1], second, ds.at[3, 1, 1], dr.at[0, z, 1], net.across))
+
+        def down_fan(zz, act):
+            first, second = down_refs(zz)
+            for kind, when, to in ways(zz):
+                pl.when(when & home)(lambda: act(put(first, first, ds.at[kind, zz, 0], dr.at[0, zz, 0], to)))
+                pl.when(when)(lambda: act(put(second, second, ds.at[kind, zz, 1], dr.at[0, zz, 1], to)))
+            pl.when(home)(lambda: act(put(first, first, ds.at[2, zz, 0], dr.at[1, zz, 0], net.across)))
+
+        def down_wait(zz, part, kind):
+            ref = down_refs(zz)[part]
+            put(ref, ref, ds.at[0, zz, part], dr.at[kind, zz, part], net.mate).wait_recv()
+
+        def from_line(k, act):
+            for way in (-1, 1):
+                zz = z + way * k
+                pl.when((zz >= 0) & (zz < line))(lambda: act(zz))
+
+        start, done = (lambda copy: copy.start()), (lambda copy: copy.wait_send())
+        net.greet((net.across, net.mate, net.diagonal))
+        own_q, own_o = attn_refs(z, x, c)
+        local = [
+            pltpu.make_async_copy(attn.at[pl.ds(0, qw)], own_q, ls.at[0]),
+            pltpu.make_async_copy(attn.at[pl.ds(qw, ow)], own_o, ls.at[1]),
+            pltpu.make_async_copy(gate_up, g_all.at[z * 2 + x], ls.at[2]),
+        ]
+        attn_fan(z, start, True)
+        for copy in local:
+            copy.start()
+        gate_fan(z, start, True)
+        keep = pltpu.make_async_copy(down, d_all.at[z], ls.at[3])
+        pl.when(mine & home)(lambda: keep.start())
+
+        def attn_on(zz):
+            attn_wait(zz, 0)
+            attn_fan(zz, start)
+
+        def gate_on(zz):
+            gate_wait(zz, 0)
+            gate_fan(zz, start)
+
+        def pass_on(zz):
+            attn_wait(zz, 1)
+            attn_pass(zz, start)
+
+        def down_on(zz):
+            pl.when(home)(lambda: down_wait(zz, 0, 0))
+            down_wait(zz, 1, 0)
+            down_fan(zz, start)
+
+        from_line(1, attn_on)
+        pass_on(z)
+        from_line(1, gate_on)
+        from_line(2, attn_on)
+        from_line(1, pass_on)
+        from_line(3, attn_on)
+        from_line(2, pass_on)
+        pl.when(mine)(lambda: down_first(start))
+        from_line(2, gate_on)
+        pl.when(mine & home)(lambda: keep.wait())
+        pl.when(home & jnp.logical_not(mine))(lambda: down_wait(z, 0, 0))
+        pl.when(jnp.logical_not(mine & home))(lambda: down_wait(z, 1, 0))
+        down_fan(z, start)
+        from_line(3, pass_on)
+        from_line(3, gate_on)
+        for k in range(1, line):
+            from_line(k, down_on)
+        for zz in range(line):
+            attn_wait(zz, 2)
+            attn_wait(zz, 3)
+            gate_wait(zz, 1)
+            pl.when(jnp.logical_not(home))(lambda: down_wait(zz, 0, 1))
+        for copy in local:
+            copy.wait()
+        for zz in range(line):
+            attn_fan(zz, done)
+            attn_pass(zz, done)
+            gate_fan(zz, done)
+            down_fan(zz, done)
+        pl.when(mine)(lambda: down_first(done))
+
+    anywhere = pl.BlockSpec(memory_space=pl.ANY)
+    sems = pltpu.SemaphoreType.DMA
+    return pl.pallas_call(
+        kernel,
+        in_specs=[anywhere] * 3,
+        out_specs=[anywhere] * 4,
+        out_shape=[
+            jax.ShapeDtypeStruct(shape, low)
+            for shape in (
+                (place.shards * qw, width),
+                (place.shards * ow, width),
+                (place.chips, unit, width),
+                (line, unit, width),
+            )
+        ],
+        scratch_shapes=[
+            sems((5, line, 2)),
+            sems((4, line, 2)),
+            sems((3, line)),
+            sems((2, line)),
+            sems((4, line, 2)),
+            sems((2, line, 2)),
+            sems((4,)),
+        ],
+        compiler_params=pltpu.CompilerParams(collective_id=1, has_side_effects=True),
+    )(attn_own, gate_up_own, down_own)
+
+
 def rms_norm(values, gains):
     return values * lax.rsqrt(jnp.mean(values * values, axis=-1, keepdims=True) + epsilon) * gains
 
@@ -247,34 +456,56 @@
     return gate * cdf, slope
 
 
-def column_blocks(whole, row_size, col_size):
-    rows, cols = whole.shape
-    return whole.reshape(rows // row_size, row_size, cols // col_size, col_size).transpose(2, 0, 1, 3)
-
-
-def column_full(blocks):
-    strips, count, row_size, col_size = blocks.shape
-    return blocks.transpose(1, 2, 0, 3).reshape(count * row_size, strips * col_size)
-
-
-def row_blocks(whole, row_size, col_size):
-    rows, cols = whole.shape
-    return whole.reshape(rows // row_size, row_size, cols // col_size, col_size).transpose(0, 2, 1, 3)
-
-
-def row_full(blocks):
-    strips, count, row_size, col_size = blocks.shape
-    return blocks.transpose(0, 2, 1, 3).reshape(strips * row_size, count * col_size)
-
-
-def refresh(grads, weights, left_stat, right_stat, left_root, right_root, decay_rate, step_rate):
-    def mul(spec, a, b):
-        return jnp.einsum(spec, a.astype(low), b.astype(low), preferred_element_type=full)
-
-    new_left = decay_rate * left_stat + (1.0 - decay_rate) * mul("sbij,sbkj->sbik", grads, grads)
-    new_right = decay_rate * right_stat + (1.0 - decay_rate) * mul("sbji,sbjk->sbik", grads, grads)
-    step = mul("sbij,sbjk->sbik", mul("sbij,sbjk->sbik", left_root, grads), right_root)
-    return (weights - step_rate * step, new_left, new_right)
+def refresh(grads, weight, left_stat, right_stat, left_root, right_root, rates, by_column):
+    strips, size, width = grads.shape
+    count = left_stat.shape[1]
+    rb = width // count
+
+    def kernel(rates_ref, g_ref, w_ref, l_ref, r_ref, lr_ref, rr_ref, g_out, w_out, l_out, r_out):
+        decay, rate, scale = rates_ref[0], rates_ref[1], rates_ref[2]
+        whole, steps = [], []
+        for s in range(strips):
+            grad = g_ref[s].astype(full)
+            scaled = (grad * scale).astype(low)
+            wide = dot(scaled, scaled, 0, 0)
+            tall = dot(scaled, scaled, 1, 1)
+            left, right = (wide, tall) if by_column else (tall, wide)
+            l_out[s, 0] = decay * l_ref[s, 0] + (1.0 - decay) * left
+            r_out[s, 0] = decay * r_ref[s, 0] + (1.0 - decay) * right
+            first, second = (rr_ref, lr_ref) if by_column else (lr_ref, rr_ref)
+            part = dot(first[s, 0].astype(low), scaled, 1, 0).astype(low)
+            whole.append(grad)
+            steps.append(dot(part, second[s, 0].astype(low), 1, 0))
+        grad, step = jnp.concatenate(whole, 0), jnp.concatenate(steps, 0)
+        g_out[...] = grad
+        w_out[...] = w_ref[...] - rate * step
+
+    flat = pl.BlockSpec((strips * size, rb), lambda i: (0, i))
+
+    def stat(a):
+        return pl.BlockSpec((strips, 1) + a.shape[2:], lambda i: (0, i, 0, 0))
+
+    return pl.pallas_call(
+        kernel,
+        grid=(count,),
+        in_specs=[
+            pl.BlockSpec(memory_space=pltpu.SMEM),
+            pl.BlockSpec((strips, size, rb), lambda i: (0, 0, i)),
+            flat,
+            stat(left_stat),
+            stat(right_stat),
+            stat(left_root),
+            stat(right_root),
+        ],
+        out_specs=[flat, flat, stat(left_stat), stat(right_stat)],
+        out_shape=[jax.ShapeDtypeStruct(a.shape, full) for a in (weight, weight, left_stat, right_stat)],
+        compiler_params=pltpu.CompilerParams(vmem_limit_bytes=48 * 2**20),
+        cost_estimate=pl.CostEstimate(
+            flops=4 * strips * size * width * (size + rb),
+            bytes_accessed=12 * (weight.size + left_stat.size + right_stat.size) + 2 * grads.size,
+            transcendentals=0,
+        ),
+    )(rates, grads, weight, left_stat, right_stat, left_root, right_root)
 
 
 def per_device(place, tokens, cotangent, segments, norm_gains, head_gains, *rest):
@@ -287,19 +518,24 @@
     unit = down_weight.shape[0]
 
     attn_own = jnp.concatenate([qkv_weight.T, out_weight], 0).astype(low)
-    both = place.gather_chips(attn_own)
-    mate = place.swap_core(both)
-    both = jnp.where(core == 0, jnp.stack([both, mate], 1), jnp.stack([mate, both], 1))
-    qkv_mat = both[:, :, :qw].reshape(place.shards * qw, width)
-    out_mat = both[:, :, qw:].reshape(place.shards * ow, width)
     gate_up_own = lax.dynamic_index_in_dim(
         gate_up_weight.T.astype(low).reshape(2, unit, width), par, 0, keepdims=False
     )
-    gate_up_all = place.gather_chips(gate_up_own)
+    down_own = down_weight.astype(low)
+    if place.direct:
+        qkv_mat, out_mat, gate_up_all, down_mat = gather_weights(place, attn_own, gate_up_own, down_own, qw)
+    else:
+        both = place.gather_chips(attn_own)
+        mate = place.swap_core(both)
+        both = jnp.where(core == 0, jnp.stack([both, mate], 1), jnp.stack([mate, both], 1))
+        qkv_mat = both[:, :, :qw].reshape(place.shards * qw, width)
+        out_mat = both[:, :, qw:].reshape(place.shards * ow, width)
+        gate_up_all = place.gather_chips(gate_up_own)
+        down_mat = place.gather_down(down_own)
     hidden_count = place.chips // 2 * unit
     gate_mat = gate_up_all[: place.chips // 2].reshape(hidden_count, width)
     up_mat = gate_up_all[place.chips // 2 :].reshape(hidden_count, width)
-    down_mat = place.gather_down(down_weight.astype(low)).reshape(hidden_count, width)
+    down_mat = down_mat.reshape(hidden_count, width)
 
     block_in = tokens.astype(full).reshape(groups * length, width)
     cosine, sine_part = jax.vmap(rope_tables)(segments)
@@ -387,45 +623,35 @@
     attn_part = (mine.astype(full) + place.swap_core(away).astype(full)).astype(low)
     attn_sum = place.sum_pairs(place.scatter_chips(attn_part))
     attn_sum = attn_sum.astype(full) + place.swap_rep(attn_sum).astype(full)
-    qkv_sum = attn_sum[:qw].T
-    out_sum = attn_sum[qw : qw + ow]
     gains = attn_sum[qw + ow]
     norm_gain_grad = gains[: 4 * norm_w].reshape(4, norm_w)
     head_gain_grad = gains[4 * norm_w : 4 * norm_w + 2 * head_w].reshape(2, head_w)
-    gate_up_grad = gate_up_sum.astype(full).T
-    down_grad = down_sum.astype(full)
 
     total_tokens = groups * length * place.reps * place.shards
     scale = float(total_tokens) ** (-0.5)
-    fresh, new_stats = [], []
+    grads, fresh, new_stats = [], [], []
     for at, (grad, weight, by_column) in enumerate(
         (
-            (qkv_sum, qkv_weight, True),
-            (out_sum, out_weight, False),
-            (gate_up_grad, gate_up_weight, True),
-            (down_grad, down_weight, False),
+            (attn_sum[:qw], qkv_weight, True),
+            (attn_sum[qw : qw + ow], out_weight, False),
+            (gate_up_sum, gate_up_weight, True),
+            (down_sum, down_weight, False),
         )
     ):
         left, right, left_root, right_root = stats[4 * at : 4 * at + 4]
-        cut = column_blocks if by_column else row_blocks
-        sizes = (left.shape[-1], right.shape[-1])
-        blocks, new_left, new_right = refresh(
-            cut(grad * scale, *sizes), cut(weight, *sizes), left, right, left_root, right_root, decay[at], rate[at]
+        strips = left.shape[0]
+        rates = jnp.stack([decay[at], rate[at], jnp.float32(scale)])
+        if by_column:
+            weight = weight.T
+        grad, weight, left, right = refresh(
+            grad.reshape(strips, -1, width), weight, left, right, left_root, right_root, rates, by_column
         )
-        fresh.append(column_full(blocks) if by_column else row_full(blocks))
-        new_stats += [new_left, new_right]
-    return (
-        block_output,
-        input_grad,
-        norm_gain_grad,
-        head_gain_grad,
-        qkv_sum,
-        out_sum,
-        gate_up_grad,
-        down_grad,
-        *fresh,
-        *new_stats,
-    )
+        if by_column:
+            grad, weight = grad.T, weight.T
+        grads.append(grad)
+        fresh.append(weight)
+        new_stats += [left, right]
+    return (block_output, input_grad, norm_gain_grad, head_gain_grad, *grads, *fresh, *new_stats)
 
 
 def solution(mesh):

time: 883 us -> 836 us (0.947)
  Pallas kernels: 0 us -> 229 us
  local copies, waits for them, and re-layouts: 137 us -> 66.1 us
  waiting for transfers between devices: 251 us -> 184 us
  starting transfers between devices: 134 us -> 69.9 us
  matrix products: 230 us -> 174 us
  other arithmetic: 115 us -> 104 us
    pallas_call x0 -> x5, Pallas kernels: none -> 229 us  [the longest x1 180 us: gather_weights(): pl.pallas_call(kernel, in_specs=[anywhere] * 3, out_specs=[anywhere] * 4,...]
    ppermute x57 -> x34, waiting for transfers between devices: 251 us -> 184 us  [send(): return lax.ppermute(value, AXES, pairs)]
    ppermute x57 -> x34, starting transfers between devices: 134 us -> 69.9 us  [send(): return lax.ppermute(value, AXES, pairs)]
    dot_general x12 -> x0, matrix products: 57.5 us -> none  [mul(): jnp.einsum(spec, a.astype(low), b.astype(low), preferred_element_type=full)]
    unnamed x256 -> x215, local copies, waits for them, and re-layouts: 45.9 us -> 19.9 us
    convert_element_type x8 -> x0, local copies, waits for them, and re-layouts: 19.3 us -> none  [mul(): b.astype(low)]
    reshape x4 -> x0, local copies, waits for them, and re-layouts: 11.8 us -> none  [the longest x2 7.21 us: column_blocks(): whole.reshape(rows // row_size, row_size, cols // col_size, col_size)]
    select_n x5 -> x1, other arithmetic: 9.55 us -> 0.21 us  [scatter_down(): return jnp.where(c != par, far, jnp.where(c == n % 2, own, near))]
  transfers between devices with their start and end apart: 57 -> 34, of which waited for: 25 -> 18; matrix products, arithmetic and copies ran while one was open for 35% -> 17% of each run, Pallas kernels for 0% -> 4%
where the time goes in v2:
time: 836 us; the launch traced here: 829 us
  Pallas kernels  229 us (27%)
  waiting for transfers between devices  184 us (22%)
  matrix products  174 us (21%)
  other arithmetic  104 us (12%)
  starting transfers between devices  69.9 us (8%)
  local copies, waits for them, and re-layouts  66.1 us (8%)
    ppermute x34, waiting for transfers between devices, send(): return lax.ppermute(value, AXES, pairs)  184 us
    pallas_call x1, Pallas kernels, gather_weights(): pl.pallas_call(kernel, in_specs=[anywhere] * 3, out_specs=[anywhere] * 4,...  180 us
    dot_general x15, matrix products, dot(): lax.dot_general(a, b, (((ca,), (cb,)), ((), ())), preferred_element_type=...  162 us
    ppermute x34, starting transfers between devices, send(): return lax.ppermute(value, AXES, pairs)  69.9 us
    pallas_call x4, Pallas kernels, refresh(): pl.pallas_call(kernel, grid=(count,), in_specs=[pl.BlockSpec(memory_space...  49.2 us
    unnamed x215, local copies, waits for them, and re-layouts  19.9 us
  transfers between devices with their start and end apart: 34, of which 18 were waited for; matrix products, arithmetic and copies ran while one was open for 17% of the time, Pallas kernels for 4%

profile of v2, /device:TPU:0, one launch (start us, length us, event | category | flops | bytes accessed | tf_op | source)
XLA Modules:
  0.0 828.9 jit_solution(5064722580429406922)
XLA Ops:
  11.6 179.6 %shard_map.410 = (bf16[1536,1152]{1,0:T(8,128)(2,1)}, bf16[1024,1152]{1,0:T(8,128)(2,1)}, bf16[8,432,1152]{2,1,0:T(8,128)(2,1)}, bf16[4,432,1152]{2,1,0:T(8,128)(2,1)}) custom-call(bf16[160,1152]{1,0:T(8,128)(2,1)} %pad_maximum_fusion.14.attn, bf16[432,1152]{1,0:T(8,128)(2,1)} %dynamic-slice_bitcast_fusion.7.gate_up, ...), custom_call_target="tpu_custom_call" | custom-call | tf_op jit(solution)/shard_map/pallas_call | solution.py:356
  240.1 27.1 %collective-permute-done = bf16[512,1152]{1,0:T(8,128)(2,1)S(1)} collective-permute-done((bf16[512,1152]{1,0:T(8,128)(2,1)S(1)}, bf16[512,1152]{1,0:T(8,128)(2,1)S(1)}, u32[]{:S(2)}, u32[]{:S(2)}) %collective-permute-start) | collective-permute-done | bytes 1179680 | tf_op jit(solution)/shard_map/ppermute | solution.py:49
  272.1 11.9 %fusion.97 = f32[2048,1728]{0,1:T(8,128)} fusion(bf16[1728,1152]{1,0:T(8,128)(2,1)S(1)} %bitcast.258, bf16[1024,1152]{1,0:T(8,128)(2,1)S(1)} %collective-permute-done.1, bf16[512,1152]{1,0:T(8,128)(2,1)S(1)} %collective-permute-done, bf16[512,1152]{1,0:T(8,128)(2,1)S(1)} %multiply_convert_fusion.3), kind=kOutput, calls=%fused_computation.246 | convolution fusion | flops 8167882752 | bytes 22855680 | tf_op jit(solution)/shard_map/dot_general | solution.py:23
  284.0 22.2 %multiply_convert_fusion.2 = (bf16[2048,1728]{0,1:T(8,128)(2,1)}, f32[2048,1728]{0,1:T(8,128)}) fusion(f32[2048,1728]{0,1:T(8,128)} %fusion.97, bf16[1728,1152]{1,0:T(8,128)(2,1)} %bitcast.256, bf16[1024,1152]{1,0:T(8,128)(2,1)} %copy-done.100, bf16[512,1152]{1,0:T(8,128)(2,1)} %copy-done.50, bf16[512,1152]{1,0:T(8,128)(2,1)S(1)} %multiply_convert_fusion.3), kind=kOutput, calls=%fused_computation.13 | convolution fusion | flops 8203272192 | bytes 44089344 | tf_op jit(solution)/shard_map/dot_general | solution.py:23
  306.2 14.1 %fusion.103 = f32[2048,1152]{1,0:T(8,128)S(1)} fusion(bf16[2048,1728]{0,1:T(8,128)(2,1)} %get-tuple-element.127, bf16[1728,1152]{1,0:T(8,128)(2,1)} %bitcast.279), kind=kOutput, calls=%fused_computation.252 | convolution fusion | flops 8153726976 | bytes 20496384 | tf_op jit(solution)/shard_map/dot_general | solution.py:23
  327.3 26.5 %collective-permute-done.3 = bf16[512,1152]{1,0:T(8,128)(2,1)S(1)} collective-permute-done((bf16[512,1152]{1,0:T(8,128)(2,1)S(1)}, bf16[512,1152]{1,0:T(8,128)(2,1)S(1)}, u32[]{:S(2)}, u32[]{:S(2)}) %collective-permute-start.3) | collective-permute-done | bytes 1179680 | tf_op jit(solution)/shard_map/ppermute | solution.py:49
  358.9 25.6 %collective-permute-done.4 = bf16[512,1152]{1,0:T(8,128)(2,1)S(1)} collective-permute-done((bf16[512,1152]{1,0:T(8,128)(2,1)S(1)}, bf16[512,1152]{1,0:T(8,128)(2,1)S(1)}, u32[]{:S(2)}, u32[]{:S(2)}) %collective-permute-start.4) | collective-permute-done | bytes 1179680 | tf_op jit(solution)/shard_map/ppermute | solution.py:49
  391.2 26.5 %multiply_convert_fusion = (bf16[2048,1728]{0,1:T(8,128)(2,1)}, bf16[2048,1728]{0,1:T(8,128)(2,1)}) fusion(f32[2048,1728]{0,1:T(8,128)} %fusion.97, f32[2048,1728]{0,1:T(8,128)} %get-tuple-element.128, bf16[1728,1152]{1,0:T(8,128)(2,1)} %bitcast.280, bf16[1024,1152]{1,0:T(8,128)(2,1)} %collective-permute-done.5, bf16[512,1152]{1,0:T(8,128)(2,1)} %copy-done.52, ...), kind=kOutput, calls=%fused_computation.11 | convolution fusion | flops 8263434240 | bytes 51167232 | tf_op jit(solution)/shard_map/dot_general | solution.py:23
  417.7 14.7 %fusion.104 = f32[2048,1152]{1,0:T(8,128)} fusion(bf16[2048,1728]{0,1:T(8,128)(2,1)} %get-tuple-element.82, bf16[1728,1152]{1,0:T(8,128)(2,1)S(1)} %bitcast.259), kind=kOutput, calls=%fused_computation.253 | convolution fusion | flops 8153726976 | bytes 20496384 | tf_op jit(solution)/shard_map/dot_general | solution.py:23
  432.4 14.1 %convolution_add_fusion = f32[2048,1152]{1,0:T(8,128)S(1)} fusion(f32[2048,1152]{1,0:T(8,128)} %fusion.104, bf16[2048,1728]{0,1:T(8,128)(2,1)} %get-tuple-element.81, bf16[1728,1152]{1,0:T(8,128)(2,1)S(1)} %bitcast.257), kind=kOutput, calls=%fused_computation.20 | convolution fusion | flops 8156086272 | bytes 29933568 | tf_op jit(solution)/shard_map/dot_general | solution.py:23
  448.1 14.0 %convolution_convert_fusion = bf16[1728,1152]{1,0:T(8,128)(2,1)} fusion(bf16[2048,1728]{0,1:T(8,128)(2,1)} %get-tuple-element.127, bf16[1024,1152]{1,0:T(8,128)(2,1)} %collective-permute-done.5, bf16[512,1152]{1,0:T(8,128)(2,1)S(1)} %copy-done.53, bf16[512,1152]{1,0:T(8,128)(2,1)S(1)} %copy-done.34), kind=kOutput, calls=%fused_computation.25 | convolution fusion | flops 8169873408 | bytes 15777792 | tf_op jit(solution)/shard_map/dot_general | solution.py:23
  463.4 13.2 %convolution_convert_fusion.1 = bf16[1728,1152]{1,0:T(8,128)(2,1)} fusion(bf16[2048,1728]{0,1:T(8,128)(2,1)} %get-tuple-element.81, bf16[1024,1152]{1,0:T(8,128)(2,1)S(1)} %copy-done.101, bf16[512,1152]{1,0:T(8,128)(2,1)S(1)} %copy-done.51, bf16[512,1152]{1,0:T(8,128)(2,1)S(1)} %copy-done.36), kind=kOutput, calls=%fused_computation.26 | convolution fusion | flops 8169873408 | bytes 15777792 | tf_op jit(solution)/shard_map/dot_general | solution.py:23
  476.6 12.8 %convolution_convert_fusion.2 = bf16[1728,1152]{1,0:T(8,128)(2,1)} fusion(bf16[2048,1728]{0,1:T(8,128)(2,1)} %get-tuple-element.82, bf16[1024,1152]{1,0:T(8,128)(2,1)S(1)} %copy-done.101, bf16[512,1152]{1,0:T(8,128)(2,1)S(1)} %copy-done.51, bf16[512,1152]{1,0:T(8,128)(2,1)S(1)} %copy-done.36), kind=kOutput, calls=%fused_computation.27 | convolution fusion | flops 8169873408 | bytes 15777792 | tf_op jit(solution)/shard_map/dot_general | solution.py:23
  494.6 7.2 pad_maximum_fusion.4
  511.0 9.7 %collective-permute-done.7 = bf16[512,1152]{1,0:T(8,128)(2,1)} collective-permute-done((bf16[512,1152]{1,0:T(8,128)(2,1)}, bf16[512,1152]{1,0:T(8,128)(2,1)}, u32[]{:S(2)}, u32[]{:S(2)}) %collective-permute-start.7) | collective-permute-done | bytes 1179680 | tf_op jit(solution)/shard_map/ppermute | solution.py:49
  571.4 6.8 add_convert_fusion
  578.3 18.6 %collective-permute-done.17 = bf16[4,432,1152]{2,1,0:T(8,128)(2,1)} collective-permute-done((bf16[4,432,1152]{2,1,0:T(8,128)(2,1)}, bf16[4,432,1152]{2,1,0:T(8,128)(2,1)}, u32[]{:S(2)}, u32[]{:S(2)}) %collective-permute-start.17) | collective-permute-done | bytes 3981344 | tf_op jit(solution)/shard_map/ppermute | solution.py:49
  596.8 5.2 fusion.10
  602.2 7.4 pad_maximum_fusion
  628.9 5.4 collective-permute-start.27
  652.2 10.1 %collective-permute-done.27 = bf16[432,1152]{1,0:T(8,128)(2,1)} collective-permute-done((bf16[432,1152]{1,0:T(8,128)(2,1)}, bf16[432,1152]{1,0:T(8,128)(2,1)}, u32[]{:S(2)}, u32[]{:S(2)}) %collective-permute-start.27) | collective-permute-done | bytes 995360 | tf_op jit(solution)/shard_map/ppermute | solution.py:49
  681.2 5.1 collective-permute-start.20
  693.0 8.2 collective-permute-done.9
  710.1 15.6 %collective-permute-done.10 = bf16[176,1152]{1,0:T(8,128)(2,1)S(1)} collective-permute-done((bf16[176,1152]{1,0:T(8,128)(2,1)S(1)}, bf16[176,1152]{1,0:T(8,128)(2,1)S(1)}, u32[]{:S(2)}, u32[]{:S(2)}) %collective-permute-start.10) | collective-permute-done | bytes 405536 | tf_op jit(solution)/shard_map/ppermute | solution.py:49
  736.3 8.0 collective-permute-done.13
  749.1 6.5 collective-permute-start.12
  755.7 5.1 collective-permute-done.14
  762.4 8.9 %collective-permute-done.15 = bf16[176,1152]{1,0:T(8,128)(2,1)S(1)} collective-permute-done((bf16[176,1152]{1,0:T(8,128)(2,1)S(1)}, bf16[176,1152]{1,0:T(8,128)(2,1)S(1)}, u32[]{:S(2)}, u32[]{:S(2)}) %collective-permute-start.15) | collective-permute-done | bytes 405536 | tf_op jit(solution)/shard_map/ppermute | solution.py:49
  774.6 11.2 %shard_map.414 = (f32[432,1152]{1,0:T(8,128)}, f32[432,1152]{1,0:T(8,128)}, f32[2,9,216,216]{3,2,1,0:T(8,128)}, f32[2,9,128,128]{3,2,1,0:T(8,128)}) custom-call(f32[3]{0:T(128)S(1)} %pad_maximum_fusion.15.rates_ref, bf16[2,216,1152]{2,1,0:T(8,128)(2,1)S(1)} %bitcast.236, f32[432,1152]{1,0:T(8,128)S(1)} %copy-done.1, f32[2,9,216,216]{3,2,1,0:T(8,128)} %l_ref.7, ...), custom_call_target="tpu_custom_call" | custom-call | flops 684785664 | bytes 20583936 | tf_op jit(solution)/shard_map/pallas_call | solution.py:488
  785.8 26.0 %shard_map.413 = (f32[864,1152]{1,0:T(8,128)}, f32[864,1152]{1,0:T(8,128)}, f32[2,9,128,128]{3,2,1,0:T(8,128)}, f32[2,9,432,432]{3,2,1,0:T(8,128)}) custom-call(f32[3]{0:T(128)S(1)} %pad_maximum_fusion.16.rates_ref, bf16[2,432,1152]{2,1,0:T(8,128)(2,1)S(1)} %maximum_select_fusion.g_ref, f32[864,1152]{1,0:T(8,128)} %bitcast.244, ...), custom_call_target="tpu_custom_call" | custom-call | flops 2229534720 | bytes 57784320 | tf_op jit(solution)/shard_map/pallas_call | solution.py:488
  816.6 6.0 shard_map.412
  822.7 6.0 shard_map.411
  (408 shorter events, 247.4 us)
Async XLA Ops:
  238.5 28.7 %collective-permute-start = (bf16[512,1152]{1,0:T(8,128)(2,1)S(1)}, bf16[512,1152]{1,0:T(8,128)(2,1)S(1)}, u32[]{:S(2)}, u32[]{:S(2)}) collective-permute-start(bf16[512,1152]{1,0:T(8,128)(2,1)S(1)} %multiply_convert_fusion.3), channel_id=1, source_target_pairs={{0,16},{1,17},{2,18},{3,19},{4,20},{5,21},{6,22},{7,23},{8,24},{9,... | collective-permute-start | bytes 3538952 | tf_op jit(solution)/shard_map/ppermute | solution.py:49
  325.7 28.1 %collective-permute-start.3 = (bf16[512,1152]{1,0:T(8,128)(2,1)S(1)}, bf16[512,1152]{1,0:T(8,128)(2,1)S(1)}, u32[]{:S(2)}, u32[]{:S(2)}) collective-permute-start(bf16[512,1152]{1,0:T(8,128)(2,1)S(1)} %slice.228), channel_id=1, source_target_pairs={{0,16},{1,17},{2,18},{3,19},{4,20},{5,21},{6,22},{7,23},{8,24},{9,... | collective-permute-start | bytes 3538952 | tf_op jit(solution)/shard_map/ppermute | solution.py:49
  357.4 27.2 %collective-permute-start.4 = (bf16[512,1152]{1,0:T(8,128)(2,1)S(1)}, bf16[512,1152]{1,0:T(8,128)(2,1)S(1)}, u32[]{:S(2)}, u32[]{:S(2)}) collective-permute-start(bf16[512,1152]{1,0:T(8,128)(2,1)S(1)} %get-tuple-element.93), channel_id=1, source_target_pairs={{0,16},{1,17},{2,18},{3,19},{4,20},{5,21},{6,22},{7,23},{8,24},{9,... | collective-permute-start | bytes 3538952 | tf_op jit(solution)/shard_map/ppermute | solution.py:49
  386.3 4.9 collective-permute-start.5
  446.8 42.6 %collective-permute-start.6 = (bf16[1024,1152]{1,0:T(8,128)(2,1)S(1)}, bf16[1024,1152]{1,0:T(8,128)(2,1)S(1)}, u32[]{:S(2)}, u32[]{:S(2)}) collective-permute-start(bf16[1024,1152]{1,0:T(8,128)(2,1)S(1)} %slice.225), channel_id=1, source_target_pairs={{0,1},{1,0},{2,3},{3,2},{4,5},{5,4},{6,7},{7,6},{8,9},{9,8},{10,11... | collective-permute-start | bytes 7077896 | tf_op jit(solution)/shard_map/ppermute | solution.py:49
  462.1 109.4 %collective-permute-start.25 = (bf16[4,432,1152]{2,1,0:T(8,128)(2,1)}, bf16[4,432,1152]{2,1,0:T(8,128)(2,1)}, u32[]{:S(2)}, u32[]{:S(2)}) collective-permute-start(bf16[4,432,1152]{2,1,0:T(8,128)(2,1)} %bitcast.74), channel_id=1, source_target_pairs={{1,3},{2,0},{5,7},{6,4},{9,11},{10,8},{13,15},{14,12},{17,19},{18,... | collective-permute-start | bytes 11943944 | tf_op jit(solution)/shard_map/ppermute | solution.py:49
  493.1 27.6 %collective-permute-start.7 = (bf16[512,1152]{1,0:T(8,128)(2,1)}, bf16[512,1152]{1,0:T(8,128)(2,1)}, u32[]{:S(2)}, u32[]{:S(2)}) collective-permute-start(bf16[512,1152]{1,0:T(8,128)(2,1)} %slice.227), channel_id=1, source_target_pairs={{0,16},{1,17},{2,18},{3,19},{4,20},{5,21},{6,22},{7,23},{8,24},{9,... | collective-permute-start | bytes 3538952 | tf_op jit(solution)/shard_map/ppermute | solution.py:49
  506.4 90.4 %collective-permute-start.17 = (bf16[4,432,1152]{2,1,0:T(8,128)(2,1)}, bf16[4,432,1152]{2,1,0:T(8,128)(2,1)}, u32[]{:S(2)}, u32[]{:S(2)}) collective-permute-start(bf16[4,432,1152]{2,1,0:T(8,128)(2,1)} %dynamic-slice_bitcast_fusion), channel_id=1, source_target_pairs={{0,2},{1,3},{2,0},{3,1},{4,6},{5,7},{6,4},{7,5},{8,10},{9,11},{10,... | collective-permute-start | bytes 11943944 | tf_op jit(solution)/shard_map/ppermute | solution.py:49
  611.2 15.0 %collective-permute-start.26 = (bf16[432,1152]{1,0:T(8,128)(2,1)}, bf16[432,1152]{1,0:T(8,128)(2,1)}, u32[]{:S(2)}, u32[]{:S(2)}) collective-permute-start(bf16[432,1152]{1,0:T(8,128)(2,1)} %get-tuple-element.85), channel_id=1, source_target_pairs={{0,4},{3,7},{4,8},{7,11},{8,12},{11,15},{16,20},{19,23},{20,24},{2... | collective-permute-start | bytes 2985992 | tf_op jit(solution)/shard_map/ppermute | solution.py:49
  616.3 49.9 %collective-permute-start.8 = (bf16[8,176,1152]{2,1,0:T(8,128)(2,1)}, bf16[8,176,1152]{2,1,0:T(8,128)(2,1)}, u32[]{:S(2)}, u32[]{:S(2)}) collective-permute-start(bf16[8,176,1152]{2,1,0:T(8,128)(2,1)} %dynamic-slice_bitcast_fusion.1), channel_id=1, source_target_pairs={{0,1},{1,0},{2,3},{3,2},{4,5},{5,4},{6,7},{7,6},{8,9},{9,8},{10,11... | collective-permute-start | bytes 9732104 | tf_op jit(solution)/shard_map/ppermute | solution.py:49
  620.4 25.5 %collective-permute-start.18 = (bf16[432,1152]{1,0:T(8,128)(2,1)}, bf16[432,1152]{1,0:T(8,128)(2,1)}, u32[]{:S(2)}, u32[]{:S(2)}) collective-permute-start(bf16[432,1152]{1,0:T(8,128)(2,1)} %get-tuple-element.89), channel_id=1, source_target_pairs={{0,4},{1,5},{2,6},{3,7},{4,8},{5,9},{6,10},{7,11},{8,12},{9,13},{1... | collective-permute-start | bytes 2985992 | tf_op jit(solution)/shard_map/ppermute | solution.py:49
  622.8 29.4 %collective-permute-start.29 = (bf16[432,1152]{1,0:T(8,128)(2,1)}, bf16[432,1152]{1,0:T(8,128)(2,1)}, u32[]{:S(2)}, u32[]{:S(2)}) collective-permute-start(bf16[432,1152]{1,0:T(8,128)(2,1)} %get-tuple-element.86), channel_id=1, source_target_pairs={{4,0},{7,3},{8,4},{11,7},{12,8},{15,11},{20,16},{23,19},{24,20},{2... | collective-permute-start | bytes 2985992 | tf_op jit(solution)/shard_map/ppermute | solution.py:49
  628.9 33.5 %collective-permute-start.27 = (bf16[432,1152]{1,0:T(8,128)(2,1)}, bf16[432,1152]{1,0:T(8,128)(2,1)}, u32[]{:S(2)}, u32[]{:S(2)}) collective-permute-start(bf16[432,1152]{1,0:T(8,128)(2,1)} %fusion.33), channel_id=1, source_target_pairs={{0,4},{3,7},{4,8},{7,11},{8,12},{11,15},{16,20},{19,23},{20,24},{2... | collective-permute-start | bytes 2985992 | tf_op jit(solution)/shard_map/ppermute | solution.py:49
  640.3 33.3 %collective-permute-start.21 = (bf16[432,1152]{1,0:T(8,128)(2,1)}, bf16[432,1152]{1,0:T(8,128)(2,1)S(1)}, u32[]{:S(2)}, u32[]{:S(2)}) collective-permute-start(bf16[432,1152]{1,0:T(8,128)(2,1)} %get-tuple-element.90), channel_id=1, source_target_pairs={{4,0},{5,1},{6,2},{7,3},{8,4},{9,5},{10,6},{11,7},{12,8},{13,9},{1... | collective-permute-start | bytes 2985992 | tf_op jit(solution)/shard_map/ppermute | solution.py:49
  647.7 30.1 %collective-permute-start.19 = (bf16[432,1152]{1,0:T(8,128)(2,1)S(1)}, bf16[432,1152]{1,0:T(8,128)(2,1)S(1)}, u32[]{:S(2)}, u32[]{:S(2)}) collective-permute-start(bf16[432,1152]{1,0:T(8,128)(2,1)S(1)} %fusion.39), channel_id=1, source_target_pairs={{0,4},{1,5},{2,6},{3,7},{4,8},{5,9},{6,10},{7,11},{8,12},{9,13},{1... | collective-permute-start | bytes 2985992 | tf_op jit(solution)/shard_map/ppermute | solution.py:49
  664.9 25.3 %collective-permute-start.30 = (bf16[432,1152]{1,0:T(8,128)(2,1)S(1)}, bf16[432,1152]{1,0:T(8,128)(2,1)S(1)}, u32[]{:S(2)}, u32[]{:S(2)}) collective-permute-start(bf16[432,1152]{1,0:T(8,128)(2,1)S(1)} %get-tuple-element.84), channel_id=1, source_target_pairs={{4,0},{7,3},{8,4},{11,7},{12,8},{15,11},{20,16},{23,19},{24,20},{2... | collective-permute-start | bytes 2985992 | tf_op jit(solution)/shard_map/ppermute | solution.py:49
  670.1 31.1 %collective-permute-start.9 = (bf16[4,176,1152]{2,1,0:T(8,128)(2,1)S(1)}, bf16[4,176,1152]{2,1,0:T(8,128)(2,1)S(1)}, u32[]{:S(2)}, u32[]{:S(2)}) collective-permute-start(bf16[4,176,1152]{2,1,0:T(8,128)(2,1)S(1)} %dynamic-slice_bitcast_fusion.2), channel_id=1, source_target_pairs={{0,2},{1,3},{2,0},{3,1},{4,6},{5,7},{6,4},{7,5},{8,10},{9,11},{10,... | collective-permute-start | bytes 4866056 | tf_op jit(solution)/shard_map/ppermute | solution.py:49
  679.9 27.5 %collective-permute-start.22 = (bf16[432,1152]{1,0:T(8,128)(2,1)S(1)}, bf16[432,1152]{1,0:T(8,128)(2,1)S(1)}, u32[]{:S(2)}, u32[]{:S(2)}) collective-permute-start(bf16[432,1152]{1,0:T(8,128)(2,1)S(1)} %get-tuple-element.88), channel_id=1, source_target_pairs={{4,0},{5,1},{6,2},{7,3},{8,4},{9,5},{10,6},{11,7},{12,8},{13,9},{1... | collective-permute-start | bytes 2985992 | tf_op jit(solution)/shard_map/ppermute | solution.py:49
  681.2 65.6 %collective-permute-start.20 = (bf16[432,1152]{1,0:T(8,128)(2,1)S(1)}, bf16[432,1152]{1,0:T(8,128)(2,1)S(1)}, u32[]{:S(2)}, u32[]{:S(2)}) collective-permute-start(bf16[432,1152]{1,0:T(8,128)(2,1)S(1)} %get-tuple-element.87), channel_id=1, source_target_pairs={{0,4},{1,5},{2,6},{3,7},{4,8},{5,9},{6,10},{7,11},{8,12},{9,13},{1... | collective-permute-start | bytes 2985992 | tf_op jit(solution)/shard_map/ppermute | solution.py:49
  686.3 40.9 %collective-permute-start.28 = (bf16[432,1152]{1,0:T(8,128)(2,1)S(1)}, bf16[432,1152]{1,0:T(8,128)(2,1)S(1)}, u32[]{:S(2)}, u32[]{:S(2)}) collective-permute-start(bf16[432,1152]{1,0:T(8,128)(2,1)S(1)} %get-tuple-element.83), channel_id=1, source_target_pairs={{0,4},{3,7},{4,8},{7,11},{8,12},{11,15},{16,20},{19,23},{20,24},{2... | collective-permute-start | bytes 2985992 | tf_op jit(solution)/shard_map/ppermute | solution.py:49
  691.7 40.5 %collective-permute-start.31 = (bf16[432,1152]{1,0:T(8,128)(2,1)S(1)}, bf16[432,1152]{1,0:T(8,128)(2,1)S(1)}, u32[]{:S(2)}, u32[]{:S(2)}) collective-permute-start(bf16[432,1152]{1,0:T(8,128)(2,1)S(1)} %fusion.32), channel_id=1, source_target_pairs={{4,0},{7,3},{8,4},{11,7},{12,8},{15,11},{20,16},{23,19},{24,20},{2... | collective-permute-start | bytes 2985992 | tf_op jit(solution)/shard_map/ppermute | solution.py:49
  702.4 23.3 %collective-permute-start.10 = (bf16[176,1152]{1,0:T(8,128)(2,1)S(1)}, bf16[176,1152]{1,0:T(8,128)(2,1)S(1)}, u32[]{:S(2)}, u32[]{:S(2)}) collective-permute-start(bf16[176,1152]{1,0:T(8,128)(2,1)S(1)} %get-tuple-element.97), channel_id=1, source_target_pairs={{0,4},{1,5},{2,6},{3,7},{4,8},{5,9},{6,10},{7,11},{8,12},{9,13},{1... | collective-permute-start | bytes 1216520 | tf_op jit(solution)/shard_map/ppermute | solution.py:49
  708.8 38.0 %collective-permute-start.23 = (bf16[432,1152]{1,0:T(8,128)(2,1)S(1)}, bf16[432,1152]{1,0:T(8,128)(2,1)S(1)}, u32[]{:S(2)}, u32[]{:S(2)}) collective-permute-start(bf16[432,1152]{1,0:T(8,128)(2,1)S(1)} %fusion.38), channel_id=1, source_target_pairs={{4,0},{5,1},{6,2},{7,3},{8,4},{9,5},{10,6},{11,7},{12,8},{13,9},{1... | collective-permute-start | bytes 2985992 | tf_op jit(solution)/shard_map/ppermute | solution.py:49
  725.8 18.5 %collective-permute-start.13 = (bf16[176,1152]{1,0:T(8,128)(2,1)S(1)}, bf16[176,1152]{1,0:T(8,128)(2,1)S(1)}, u32[]{:S(2)}, u32[]{:S(2)}) collective-permute-start(bf16[176,1152]{1,0:T(8,128)(2,1)S(1)} %get-tuple-element.98), channel_id=1, source_target_pairs={{4,0},{5,1},{6,2},{7,3},{8,4},{9,5},{10,6},{11,7},{12,8},{13,9},{1... | collective-permute-start | bytes 1216520 | tf_op jit(solution)/shard_map/ppermute | solution.py:49
  727.2 17.9 %collective-permute-start.11 = (bf16[176,1152]{1,0:T(8,128)(2,1)S(1)}, bf16[176,1152]{1,0:T(8,128)(2,1)S(1)}, u32[]{:S(2)}, u32[]{:S(2)}) collective-permute-start(bf16[176,1152]{1,0:T(8,128)(2,1)S(1)} %fusion.54), channel_id=1, source_target_pairs={{0,4},{1,5},{2,6},{3,7},{4,8},{5,9},{6,10},{7,11},{8,12},{9,13},{1... | collective-permute-start | bytes 1216520 | tf_op jit(solution)/shard_map/ppermute | solution.py:49
  733.8 28.4 %collective-permute-start.32 = (bf16[432,1152]{1,0:T(8,128)(2,1)S(1)}, bf16[432,1152]{1,0:T(8,128)(2,1)S(1)}, u32[]{:S(2)}, u32[]{:S(2)}) collective-permute-start(bf16[432,1152]{1,0:T(8,128)(2,1)S(1)} %fusion.36), channel_id=1, source_target_pairs={{0,16},{3,18},{4,20},{7,22},{8,24},{11,26},{12,28},{15,30},{16,1},... | collective-permute-start | bytes 2985992 | tf_op jit(solution)/shard_map/ppermute | solution.py:49
  744.3 17.9 %collective-permute-start.33 = (bf16[432,1152]{1,0:T(8,128)(2,1)S(1)}, bf16[432,1152]{1,0:T(8,128)(2,1)S(1)}, u32[]{:S(2)}, u32[]{:S(2)}) collective-permute-start(bf16[432,1152]{1,0:T(8,128)(2,1)S(1)} %fusion.36), channel_id=1, source_target_pairs={{3,2},{7,6},{11,10},{15,14},{16,17},{20,21},{24,25},{28,29}} | collective-permute-start | bytes 2985992 | tf_op jit(solution)/shard_map/ppermute | solution.py:49
  745.3 15.5 %collective-permute-start.14 = (bf16[176,1152]{1,0:T(8,128)(2,1)S(1)}, bf16[176,1152]{1,0:T(8,128)(2,1)S(1)}, u32[]{:S(2)}, u32[]{:S(2)}) collective-permute-start(bf16[176,1152]{1,0:T(8,128)(2,1)S(1)} %get-tuple-element.96), channel_id=1, source_target_pairs={{4,0},{5,1},{6,2},{7,3},{8,4},{9,5},{10,6},{11,7},{12,8},{13,9},{1... | collective-permute-start | bytes 1216520 | tf_op jit(solution)/shard_map/ppermute | solution.py:49
  748.4 25.7 %collective-permute-start.24 = (bf16[432,1152]{1,0:T(8,128)(2,1)S(1)}, bf16[432,1152]{1,0:T(8,128)(2,1)S(1)}, u32[]{:S(2)}, u32[]{:S(2)}) collective-permute-start(bf16[432,1152]{1,0:T(8,128)(2,1)S(1)} %fusion.42), channel_id=1, source_target_pairs={{0,16},{1,17},{2,18},{3,19},{4,20},{5,21},{6,22},{7,23},{8,24},{9,... | collective-permute-start | bytes 2985992 | tf_op jit(solution)/shard_map/ppermute | solution.py:49
  749.1 13.3 %collective-permute-start.12 = (bf16[176,1152]{1,0:T(8,128)(2,1)S(1)}, bf16[176,1152]{1,0:T(8,128)(2,1)S(1)}, u32[]{:S(2)}, u32[]{:S(2)}) collective-permute-start(bf16[176,1152]{1,0:T(8,128)(2,1)S(1)} %get-tuple-element.95), channel_id=1, source_target_pairs={{0,4},{1,5},{2,6},{3,7},{4,8},{5,9},{6,10},{7,11},{8,12},{9,13},{1... | collective-permute-start | bytes 1216520 | tf_op jit(solution)/shard_map/ppermute | solution.py:49
  760.9 10.4 %collective-permute-start.15 = (bf16[176,1152]{1,0:T(8,128)(2,1)S(1)}, bf16[176,1152]{1,0:T(8,128)(2,1)S(1)}, u32[]{:S(2)}, u32[]{:S(2)}) collective-permute-start(bf16[176,1152]{1,0:T(8,128)(2,1)S(1)} %fusion.53), channel_id=1, source_target_pairs={{4,0},{5,1},{6,2},{7,3},{8,4},{9,5},{10,6},{11,7},{12,8},{13,9},{1... | collective-permute-start | bytes 1216520 | tf_op jit(solution)/shard_map/ppermute | solution.py:49
  771.5 40.3 %collective-permute-start.16 = (bf16[176,1152]{1,0:T(8,128)(2,1)S(1)}, bf16[176,1152]{1,0:T(8,128)(2,1)S(1)}, u32[]{:S(2)}, u32[]{:S(2)}) collective-permute-start(bf16[176,1152]{1,0:T(8,128)(2,1)S(1)} %fusion.57), channel_id=1, source_target_pairs={{0,16},{1,17},{2,18},{3,19},{4,20},{5,21},{6,22},{7,23},{8,24},{9,... | collective-permute-start | bytes 1216520 | tf_op jit(solution)/shard_map/ppermute | solution.py:49
  (108 other events, 1526.0 us)
